TPU v7x, 1024 devices: a whole 4x4x32 slice. The times are simulated.
1024 devices in a mesh: row: 64 (over z_lo, x, core), col: 16 (over y, z_hi).
Axes of the slice: x: 4, y: 4, z: 32 (z_hi: 4, z_lo: 8; z = z_hi * 8 + z_lo), core: 2. Of those that a mesh axis runs over, the one named last changes fastest.
Arguments:
- left_blocks: bfloat16 [192, 2048, 128], P('row', 'col'), may hold values from -4 to 4
- left_index: int32 [192, 32], P('row', 'col'), may hold values from -1 to 1151, as said below
- right_blocks: bfloat16 [128, 2048, 128], P('row', 'col'), may hold values from -4 to 4
- right_index: int32 [128, 32], P('row', 'col'), may hold values from 0 to 1152, as said below
- out_pattern: int32 [128, 128], P('row', 'col'), may hold values 0 or 1
Outputs:
- product: bfloat16 [16384, 16384], P('row', 'col')
Inputs may be any that keep to these rules, and one draw needn't show every extreme that they name: `left_index`: column 0 of a left slot is a block row from 0 to 1; column 1 is a block column within the 72 columns of the device's grid column, or -1 for an empty slot. No two live slots of one grid row name the same pair. The live slots of a device come first, and some device has all 3 slots live. All block indices named by live slots of either pattern lie in one common set holding 2 of every 18 consecutive block indices. `right_index`: column 0 of a right slot is a block row within the 18 rows of the device's grid row, or 1152 for an empty slot; column 1 is a block column from 0 to 7. No two live slots of one device name the same pair. The live slots of a device come first, and some device has all 2 slots live.
All inputs are finite; a program needn't handle non-finite values. No bound on the sum of `out_pattern` on one device may be relied on, other than what follows from the above.
Results may differ from a plain program's by a relative error of at most 0.001.
Values may be sent and summed in bfloat16 or wider, within the bound.
No kernel may reach another device: no remote copies, remote signals or barrier semaphores. Data moves between devices by JAX's collectives and lax.ppermute only.
A program may use at most 32 MiB of HBM per device.

v0:
```python
import math

import jax
import jax.numpy as jnp
from jax import lax
from jax.sharding import PartitionSpec as P


def contribute(left_all, left_keys, right_all, right_keys, band, slab):
    count = right_all.shape[0]
    width = right_all.shape[-1]
    group = math.gcd(count, 32)
    band_rows = jnp.arange(band, dtype=jnp.int32)
    slot_ids = jnp.arange(left_all.shape[0], dtype=jnp.int32)
    columns = jnp.arange(slab, dtype=jnp.int32)
    blocks_grouped = right_all.reshape(count // group, group, width, width)
    keys_grouped = right_keys.reshape(count // group, group, 2)

    def step(total, pair):
        blocks, keys = pair
        match = (left_keys[None, None, :, 1] == keys[:, None, None, 0]) & (
            left_keys[None, None, :, 0] == band_rows[None, :, None]
        )
        found = jnp.any(match, axis=2)
        where = jnp.sum(jnp.where(match, slot_ids[None, None, :], 0), axis=2)
        picked = jnp.where(found[:, :, None, None], left_all[where], jnp.zeros((), left_all.dtype))
        partial_value = jnp.einsum(
            "bixy,byz->bixz", picked, blocks, preferred_element_type=jnp.float32
        )
        select = (keys[:, 1:2] == columns[None, :]).astype(jnp.float32)
        return (
            total
            + jnp.einsum("bj,bixz->ixjz", select, partial_value, precision=lax.Precision.HIGHEST),
            None,
        )

    start = jnp.zeros((band, width, slab, width), jnp.float32)
    total, unused = lax.scan(step, start, (blocks_grouped, keys_grouped))
    return total


def gather_left(left_blocks, left_index):
    return (
        lax.all_gather(left_blocks, "col", axis=0, tiled=True),
        lax.all_gather(left_index, "col", axis=0, tiled=True),
    )


def gather_right(right_blocks, right_index):
    return (
        lax.all_gather(right_blocks, "row", axis=0, tiled=True),
        lax.all_gather(right_index, "row", axis=0, tiled=True),
    )


def per_device(left_blocks, left_index, right_blocks, right_index, out_pattern):
    band = out_pattern.shape[0]
    slab = out_pattern.shape[1]
    width = left_blocks.shape[-1]
    left_all, left_keys = gather_left(left_blocks, left_index)
    right_all, right_keys = gather_right(right_blocks, right_index)
    total = contribute(left_all, left_keys, right_all, right_keys, band, slab)
    kept = jnp.where(out_pattern[:, None, :, None] > 0, total, jnp.zeros((), total.dtype))
    return kept.reshape(band * width, slab * width).astype(jnp.bfloat16)


def solution(mesh):
    placed = (
        P("row", "col", None),
        P("row", "col"),
        P("row", "col", None),
        P("row", "col"),
        P("row", "col"),
    )
    return jax.shard_map(
        per_device, mesh=mesh, in_specs=placed, out_specs=P("row", "col"), check_vma=False
    )
```

profile of v0, /device:TPU:1, one launch (start us, length us, event | category | flops | bytes accessed | tf_op | source)
XLA Modules:
  0.0 357.0 jit_solution(18290949589221835438)
XLA Ops:
  6.5 0.7 all-gather.5.cloned.1.call-update
  7.3 0.7 all-gather.7.cloned.1.call-update
  8.0 129.3 %all-gather.1 = s32[64,2,2]{2,1,0:T(2,128)S(1)} all-gather(s32[1,2,2]{2,1,0:T(2,128)} %bitcast.61), channel_id=1, replica_groups=mesh['row'=64,'col'=16] {'row'}, dimensions={0}, use_global_device_ids=true | all-gather | bytes 1040 | tf_op jit(solution)/shard_map/all_gather | solution.py:52
  137.4 84.5 %all-gather = s32[16,3,2]{1,2,0:T(2,128)S(1)} all-gather(s32[1,3,2]{1,2,0:T(2,128)} %bitcast.62), channel_id=1, replica_groups=mesh['row'=64,'col'=16] {'col'}, dimensions={0}, use_global_device_ids=true | all-gather | bytes 408 | tf_op jit(solution)/shard_map/all_gather | solution.py:45
  222.0 0.7 broadcast_compare_fusion.1
  222.7 73.4 %all-gather.7.cloned.1.call-done = bf16[128,128,128]{2,1,0:T(8,128)(2,1)} async-done(((bf16[2,128,128]{2,1,0:T(8,128)(2,1)}), bf16[128,128,128]{2,1,0:T(8,128)(2,1)}) %all-gather.7.cloned.1.call-update) | async-done | bytes 4194320 | tf_op jit(solution)/shard_map/all_gather | solution.py:51
  296.0 53.0 %while.11 = (s32[]{:T(128)}, f32[2,128,8,128]{3,2,1,0:T(8,128)S(1)}, s32[48,2]{0,1:T(2,128)S(1)}, s32[4,32,2]{1,2,0:T(2,128)S(1)}, bf16[48,128,128]{2,1,0:T(8,12...) while((s32[]{:T(128)}, f32[2,128,8,128]{3,2,1,0:T(8,128)S(1)}, ...), condition=%wide.region_3.4_spmd.clone, body=%wide.region_0.3_spmd.clone.sunk | while | flops 370689952 | bytes 17840388 | solution.py:38
  296.1 0.1 fusion.37
  296.4 0.1 reshape.121
  296.5 2.4 gather_fusion
  298.8 0.1 and_reduce_fusion.2
  299.1 4.0 %fusion.38 = f32[32,2,128,128]{3,2,1,0:T(8,128)} fusion(bf16[32,2,128,128]{3,2,1,0:T(8,128)(2,1)S(1)} %bitcast.57, pred[32,2]{1,0:T(8,128)(4,1)S(1)} %copy.37, bf16[4,32,128,128]{3,2,1,0:T(8,128)(2,1)} %get-tuple-element.186, s32[]{:T(128)} %get-tuple-element.173), kind=kOutput, calls=%fused_computation.6.clone.1 | convolution fusion | flops 269484032 | bytes 7340608 | tf_op jit(solution)/shard_map/while/body/eval_jaxpr/bixy,byz->bixz/dot_general | solution.py:27
  303.0 6.2 %fusion.39 = f32[2,128,8,128]{3,2,1,0:T(8,128)S(1)} fusion(f32[32,2,128,128]{3,2,1,0:T(8,128)} %fusion.38, f32[2,128,8,128]{3,2,1,0:T(8,128)S(1)} %get-tuple-element.174, pred[]{:T(512)S(6)} %compare.3, s32[32]{0:T(128)S(1)} %get-tuple-element.164), kind=kOutput, calls=%fused_computation.10.clone.1 | convolution fusion | flops 101187840 | bytes 6291585 | tf_op jit(solution)/shard_map/while/body/eval_jaxpr/bj,bixz->ixjz/dot_general | solution.py:33
  309.4 0.1 fusion.37
  309.6 0.1 reshape.121
  309.7 2.4 gather_fusion
  312.1 0.1 and_reduce_fusion.2
  312.3 4.0 %fusion.38 = f32[32,2,128,128]{3,2,1,0:T(8,128)} fusion(bf16[32,2,128,128]{3,2,1,0:T(8,128)(2,1)S(1)} %bitcast.57, pred[32,2]{1,0:T(8,128)(4,1)S(1)} %copy.37, bf16[4,32,128,128]{3,2,1,0:T(8,128)(2,1)} %get-tuple-element.186, s32[]{:T(128)} %get-tuple-element.173), kind=kOutput, calls=%fused_computation.6.clone.1 | convolution fusion | flops 269484032 | bytes 7340608 | tf_op jit(solution)/shard_map/while/body/eval_jaxpr/bixy,byz->bixz/dot_general | solution.py:27
  316.3 6.2 %fusion.39 = f32[2,128,8,128]{3,2,1,0:T(8,128)S(1)} fusion(f32[32,2,128,128]{3,2,1,0:T(8,128)} %fusion.38, f32[2,128,8,128]{3,2,1,0:T(8,128)S(1)} %get-tuple-element.174, pred[]{:T(512)S(6)} %compare.3, s32[32]{0:T(128)S(1)} %get-tuple-element.164), kind=kOutput, calls=%fused_computation.10.clone.1 | convolution fusion | flops 101187840 | bytes 6291585 | tf_op jit(solution)/shard_map/while/body/eval_jaxpr/bj,bixz->ixjz/dot_general | solution.py:33
  322.7 0.1 fusion.37
  322.9 0.1 reshape.121
  323.0 2.4 gather_fusion
  325.4 0.1 and_reduce_fusion.2
  325.6 4.0 %fusion.38 = f32[32,2,128,128]{3,2,1,0:T(8,128)} fusion(bf16[32,2,128,128]{3,2,1,0:T(8,128)(2,1)S(1)} %bitcast.57, pred[32,2]{1,0:T(8,128)(4,1)S(1)} %copy.37, bf16[4,32,128,128]{3,2,1,0:T(8,128)(2,1)} %get-tuple-element.186, s32[]{:T(128)} %get-tuple-element.173), kind=kOutput, calls=%fused_computation.6.clone.1 | convolution fusion | flops 269484032 | bytes 7340608 | tf_op jit(solution)/shard_map/while/body/eval_jaxpr/bixy,byz->bixz/dot_general | solution.py:27
  329.6 6.2 %fusion.39 = f32[2,128,8,128]{3,2,1,0:T(8,128)S(1)} fusion(f32[32,2,128,128]{3,2,1,0:T(8,128)} %fusion.38, f32[2,128,8,128]{3,2,1,0:T(8,128)S(1)} %get-tuple-element.174, pred[]{:T(512)S(6)} %compare.3, s32[32]{0:T(128)S(1)} %get-tuple-element.164), kind=kOutput, calls=%fused_computation.10.clone.1 | convolution fusion | flops 101187840 | bytes 6291585 | tf_op jit(solution)/shard_map/while/body/eval_jaxpr/bj,bixz->ixjz/dot_general | solution.py:33
  335.9 0.1 fusion.37
  336.3 2.4 gather_fusion
  338.6 0.1 and_reduce_fusion.2
  338.9 4.0 %fusion.38 = f32[32,2,128,128]{3,2,1,0:T(8,128)} fusion(bf16[32,2,128,128]{3,2,1,0:T(8,128)(2,1)S(1)} %bitcast.57, pred[32,2]{1,0:T(8,128)(4,1)S(1)} %copy.37, bf16[4,32,128,128]{3,2,1,0:T(8,128)(2,1)} %get-tuple-element.186, s32[]{:T(128)} %get-tuple-element.173), kind=kOutput, calls=%fused_computation.6.clone.1 | convolution fusion | flops 269484032 | bytes 7340608 | tf_op jit(solution)/shard_map/while/body/eval_jaxpr/bixy,byz->bixz/dot_general | solution.py:27
  342.8 6.2 %fusion.39 = f32[2,128,8,128]{3,2,1,0:T(8,128)S(1)} fusion(f32[32,2,128,128]{3,2,1,0:T(8,128)} %fusion.38, f32[2,128,8,128]{3,2,1,0:T(8,128)S(1)} %get-tuple-element.174, pred[]{:T(512)S(6)} %compare.3, s32[32]{0:T(128)S(1)} %get-tuple-element.164), kind=kOutput, calls=%fused_computation.10.clone.1 | convolution fusion | flops 101187840 | bytes 6291585 | tf_op jit(solution)/shard_map/while/body/eval_jaxpr/bj,bixz->ixjz/dot_general | solution.py:33
  349.1 0.2 select_convert_fusion
  349.2 0.9 copy.31
  (44 shorter events, 1.6 us)
Async XLA Ops:
  6.5 216.2 %all-gather.5.cloned.1.call-start = ((), (), s32[]{:S(2)}) async-start(), calls=%async_computation | async-start | bytes 1671168 | tf_op jit(solution)/shard_map/all_gather | solution.py:44
  7.3 288.8 %all-gather.7.cloned.1.call-start = ((), (), s32[]{:S(2)}) async-start(), calls=%async_computation.1 | async-start | bytes 4259840 | tf_op jit(solution)/shard_map/all_gather | solution.py:51
Sparse Core Ops, SparseCore 0:
  11.6 160.5 all-gather.4
  174.9 121.1 all-gather.6
where the time goes:
time: 358 us; the launch traced here: 357 us
  blocking collectives  214 us (60%)
  waiting for transfers between devices  74.8 us (21%)
  matrix products  40.8 us (11%)
  between operations  13.4 us (4%)
  local copies, waits for them, and re-layouts  11.8 us (3%)
    all_gather x1, blocking collectives, gather_right(): lax.all_gather(right_index, 'row', axis=0, tiled=True)  129 us
    all_gather x1, blocking collectives, gather_left(): lax.all_gather(left_index, 'col', axis=0, tiled=True)  84.5 us
    all_gather x1, waiting for transfers between devices, gather_right(): lax.all_gather(right_blocks, 'row', axis=0, tiled=True)  73.4 us
    dot_general x4, matrix products, step(): jnp.einsum('bj,bixz->ixjz', select, partial_value, precision=lax.Precisio...  24.9 us
    dot_general x4, matrix products, step(): jnp.einsum('bixy,byz->bixz', picked, blocks, preferred_element_type=jnp.f...  15.8 us
    gather x4, local copies, waits for them, and re-layouts, step(): left_all[where]  9.43 us
  transfers between devices with their start and end apart: 2, of which 1 were waited for; matrix products, arithmetic and copies ran while one was open for 0% of the time, Pallas kernels for 0%

commit v1 on v0

v1 whole, which is shorter than its diff:
```python
import jax
import jax.numpy as jnp
from jax import lax
from jax.experimental import pallas as pl
from jax.experimental.pallas import tpu as pltpu
from jax.sharding import PartitionSpec as P

Z_LO, X, CORE, Y, Z_HI = 8, 4, 2, 4, 4
BLK = 128
HOLD = 10**11
META = 16
A_SLOTS, B_SLOTS = 3, 2
A_ROWS = A_SLOTS * BLK + META
B_ROWS = B_SLOTS * BLK + META
K_COL = 72
K_ROW = 18


def pairs(partner):
    out = []
    for zl in range(Z_LO):
        for x in range(X):
            for q in range(CORE):
                for y in range(Y):
                    for zh in range(Z_HI):
                        a, b, c, d, e = partner(zl, x, q, y, zh)
                        out.append(
                            (
                                (((zl * X + x) * CORE + q) * Y + y) * Z_HI + zh,
                                (((a * X + b) * CORE + c) * Y + d) * Z_HI + e,
                            )
                        )
    return out


def swap(value, partner):
    return lax.ppermute(value, ("row", "col"), pairs(partner))


def z_lo_swap(value, d):
    return swap(value, lambda zl, x, q, y, zh: (zl ^ d, x, q, y, zh))


def z_hi_swap(value, first, second):
    return swap(value, lambda zl, x, q, y, zh: (zl, x, q, y, zh ^ (second if q else first)))


def y_swap(value, first, second):
    return swap(value, lambda zl, x, q, y, zh: (zl, x, q, y ^ (second if q else first), zh))


def x_swap(value, first, second):
    return swap(value, lambda zl, x, q, y, zh: (zl, x ^ (second if q else first), q, y, zh))


def core_swap(value):
    return swap(value, lambda zl, x, q, y, zh: (zl, x, q ^ 1, y, zh))


def after(value, *others):
    return lax.optimization_barrier((value, *others))[0]


def hold(value, flops=HOLD):
    def kernel(in_ref, out_ref):
        out_ref[...] = in_ref[...]

    return pl.pallas_call(
        kernel,
        out_shape=jax.ShapeDtypeStruct(value.shape, value.dtype),
        cost_estimate=pl.CostEstimate(flops=flops, bytes_accessed=0, transcendentals=0),
        name="hold",
    )(value)


def meta_rows(values):
    flat = jnp.concatenate(values).astype(jnp.bfloat16)
    return jnp.pad(flat[None, :], ((0, META - 1), (0, BLK - flat.shape[0])))


def gather(left, right):
    rows = A_ROWS
    cat = jnp.concatenate
    sibling = core_swap(left)
    right = cat([right, z_lo_swap(right, 4)])
    z_one = z_hi_swap(cat([left, sibling]), 1, 3)
    right = cat([right, z_lo_swap(right, 2)])
    z_one_mine = hold(z_one[:rows])
    right = cat([right, z_lo_swap(right, 1)])
    high = right.shape[0]
    z_two = z_hi_swap(z_one_mine, 3, 1)
    swapped = core_swap(cat([right, z_one_mine, z_one[rows:]]))
    near_right, z_other = swapped[:high], swapped[high:]
    x_one = x_swap(cat([right, near_right]), 1, 3)
    mine = cat([left, z_one_mine, z_other[rows:]])
    others = cat([sibling, z_one[rows:], z_other[:rows]])
    y_one = y_swap(cat([mine, others]), 1, 3)
    x_two = x_swap(x_one[:high], 3, 1)
    z_two = hold(z_two)
    y_two = y_swap(cat([y_one[: 3 * rows], z_two]), 3, 1)
    y_last = [y_swap(z_two, 1, 3), y_swap(z_two, 2, 2)]
    swapped = core_swap(cat([x_one, y_one[3 * rows :]]))
    x_two, y_two = lax.optimization_barrier((x_two, y_two))
    x_last = core_swap(x_two)
    return (
        [mine, y_one[: 3 * rows], y_two, swapped[2 * high :], z_two] + y_last,
        [right, near_right, x_one, swapped[: 2 * high], x_two, x_last],
    )


def product_kernel(n_left, n_right, place_ref, pattern_ref, *refs):
    left_parts = refs[:n_left]
    right_parts = refs[n_left : n_left + n_right]
    out_ref = refs[n_left + n_right]
    left, right, total, left_meta, right_meta, left_keys, right_keys, work, sems, key_sems = refs[
        n_left + n_right + 1 :
    ]
    copies = []
    for parts, held in ((left_parts, left), (right_parts, right)):
        at = 0
        for part in parts:
            copy = pltpu.make_async_copy(
                part, held.at[pl.ds(at, part.shape[0])], sems.at[len(copies)]
            )
            copy.start()
            copies.append(copy)
            at += part.shape[0]
    total[...] = jnp.zeros_like(total)
    for copy in copies:
        copy.wait()
    n_a = left_meta.shape[0]
    n_b = right_meta.shape[0]
    for i in range(n_a):
        rows = left[pl.ds(i * A_ROWS + A_SLOTS * BLK, META), :].astype(jnp.float32)
        left_meta[pl.ds(i, 1), :] = rows[0:1].astype(jnp.int32)
    for i in range(n_b):
        rows = right[pl.ds(i * B_ROWS + B_SLOTS * BLK, META), :].astype(jnp.float32)
        right_meta[pl.ds(i, 1), :] = rows[0:1].astype(jnp.int32)
    left_copy = pltpu.make_async_copy(left_meta, left_keys, key_sems.at[0])
    right_copy = pltpu.make_async_copy(right_meta, right_keys, key_sems.at[1])
    left_copy.start()
    right_copy.start()
    left_copy.wait()
    right_copy.wait()

    row = place_ref[0]
    col = place_ref[1]
    zl, x, q = row // (X * CORE), (row // CORE) % X, row % CORE
    y, zh = col // Z_HI, col % Z_HI
    near, far = jnp.where(q == 0, 1, 3), jnp.where(q == 0, 3, 1)

    def shard(i, count):
        n = jnp.where(i < 9, i, i - 1)
        p, r = n % 3, n // 3
        dz = jnp.where(p == 0, 0, jnp.where((p == 1) == (r < 3), near, far))
        dy = jnp.where(r == 0, 0, jnp.where(r == 1, near, jnp.where(r == 2, 2, far)))
        opposite = (i == 9) | (i > 12)
        dz = jnp.where(opposite, 2, dz)
        dy = jnp.where(
            opposite,
            jnp.where(i == 9, far, jnp.where(i == 13, 0, jnp.where(i == 14, near, 2))),
            dy,
        )
        there = (y ^ dy) * Z_HI + (zh ^ dz)

        def slot(s, count):
            offset = left_keys[i, s]
            band = left_keys[i, A_SLOTS + s]
            live = offset >= 0
            inside = jnp.maximum(offset, 0)
            group = inside // K_ROW
            want = inside - group * K_ROW
            other = there * (K_COL // K_ROW) + group
            e = (other % CORE) ^ q
            u = ((other // CORE) % X) ^ x
            w = (other // (X * CORE)) ^ zl
            m = ((w & 1) << 2) | (w & 2) | (w >> 2)
            part = jnp.where(
                u == 0,
                e,
                jnp.where(u == 2, 6 + e, jnp.where(u == near, 2 + e, 5 - e)),
            )
            t = part * Z_LO + m
            for j in range(B_SLOTS):
                column = right_keys[t, B_SLOTS + j]
                hit = live & (right_keys[t, j] == want) & (pattern_ref[band, column] > 0)

                @pl.when(hit)
                def _():
                    work[0, count] = i * A_ROWS + s * BLK
                    work[1, count] = t * B_ROWS + j * BLK
                    work[2, count] = band * pattern_ref.shape[1] + column

                count = count + hit.astype(jnp.int32)
            return count

        for s in range(A_SLOTS):
            count = slot(s, count)
        return count

    count = lax.fori_loop(0, n_a, shard, jnp.int32(0))

    def multiply(n, carry):
        a = left[pl.ds(pl.multiple_of(work[0, n], 16), BLK), :]
        b = right[pl.ds(pl.multiple_of(work[1, n], 16), BLK), :]
        total[work[2, n]] += jnp.dot(a, b, preferred_element_type=jnp.float32)
        return carry

    lax.fori_loop(0, count, multiply, 0)
    band, slab = pattern_ref.shape
    for i in range(band):
        for j in range(slab):
            out_ref[i * BLK : (i + 1) * BLK, j * BLK : (j + 1) * BLK] = total[i * slab + j].astype(
                out_ref.dtype
            )


def multiply_parts(left_parts, right_parts, row, col, pattern):
    band, slab = pattern.shape
    n_a = sum(p.shape[0] for p in left_parts) // A_ROWS
    n_b = sum(p.shape[0] for p in right_parts) // B_ROWS
    n_parts = len(left_parts) + len(right_parts)
    smem = pl.BlockSpec(memory_space=pltpu.SMEM)
    anywhere = pl.BlockSpec(memory_space=pl.ANY)
    place = jnp.stack([row, col]).astype(jnp.int32)

    def kernel(*refs):
        product_kernel(len(left_parts), len(right_parts), *refs)

    return pl.pallas_call(
        kernel,
        out_shape=jax.ShapeDtypeStruct((band * BLK, slab * BLK), jnp.bfloat16),
        in_specs=[smem, smem] + [anywhere] * n_parts,
        out_specs=pl.BlockSpec(memory_space=pltpu.VMEM),
        scratch_shapes=[
            pltpu.VMEM((n_a * A_ROWS, BLK), jnp.bfloat16),
            pltpu.VMEM((n_b * B_ROWS, BLK), jnp.bfloat16),
            pltpu.VMEM((band * slab, BLK, BLK), jnp.float32),
            pltpu.VMEM((n_a, BLK), jnp.int32),
            pltpu.VMEM((n_b, BLK), jnp.int32),
            pltpu.SMEM((n_a, BLK), jnp.int32),
            pltpu.SMEM((n_b, BLK), jnp.int32),
            pltpu.SMEM((3, n_a * A_SLOTS * B_SLOTS), jnp.int32),
            pltpu.SemaphoreType.DMA((n_parts,)),
            pltpu.SemaphoreType.DMA((2,)),
        ],
        compiler_params=pltpu.CompilerParams(vmem_limit_bytes=24 * 1024 * 1024),
        name="block_products",
    )(place, pattern, *left_parts, *right_parts)


def per_device(left_blocks, left_index, right_blocks, right_index, out_pattern):
    row = lax.axis_index("row")
    col = lax.axis_index("col")
    offset = jnp.where(left_index[:, 1] >= 0, left_index[:, 1] - col * K_COL, -1)
    left = jnp.concatenate(
        [left_blocks.reshape(-1, BLK), meta_rows([offset, left_index[:, 0]])]
    )
    live = right_index[:, 0] < (row + 1) * K_ROW
    offset = jnp.where(live, right_index[:, 0] - row * K_ROW, -1)
    right = jnp.concatenate(
        [right_blocks.reshape(-1, BLK), meta_rows([offset, jnp.where(live, right_index[:, 1], 0)])]
    )
    return multiply_parts(*gather(left, right), row, col, out_pattern)


def solution(mesh):
    placed = (
        P("row", "col", None),
        P("row", "col"),
        P("row", "col", None),
        P("row", "col"),
        P("row", "col"),
    )
    return jax.shard_map(
        per_device, mesh=mesh, in_specs=placed, out_specs=P("row", "col"), check_vma=False
    )
```

time: 358 us -> 141 us (0.39)
  blocking collectives: 214 us -> 0 us
  starting transfers between devices: 0.04 us -> 70.9 us
  matrix products: 40.8 us -> 0 us
  waiting for transfers between devices: 74.8 us -> 38.9 us
  Pallas kernels: 0 us -> 13.4 us
  between operations: 13.4 us -> 0.32 us
  other arithmetic: 2.16 us -> 7.08 us
    all_gather x2 -> x0, blocking collectives: 214 us -> none  [the longest x1 129 us: gather_right(): lax.all_gather(right_index, 'row', axis=0, tiled=True)]
    all_gather x2 -> x0, waiting for transfers between devices: 73.4 us -> none  [the longest x1 73.4 us: gather_right(): lax.all_gather(right_blocks, 'row', axis=0, tiled=True)]
    ppermute x0 -> x15, starting transfers between devices: none -> 70.9 us  [swap(): return lax.ppermute(value, ('row', 'col'), pairs(partner))]
    dot_general x8 -> x0, matrix products: 40.8 us -> none  [the longest x4 24.9 us: step(): jnp.einsum('bj,bixz->ixjz', select, partial_value, precision=lax.Precisio...]
    ppermute x0 -> x15, waiting for transfers between devices: none -> 38.9 us  [swap(): return lax.ppermute(value, ('row', 'col'), pairs(partner))]
    pallas_call x0 -> x3, Pallas kernels: none -> 13.4 us  [the longest x1 10.3 us: multiply_parts(): pl.pallas_call(kernel, out_shape=jax.ShapeDtypeStruct((band * BLK, slab *...]
    gather x4 -> x0, local copies, waits for them, and re-layouts: 9.43 us -> none  [step(): left_all[where]]
    concatenate x0 -> x9, other arithmetic: none -> 4.58 us  [the longest x1 1.21 us: gather(): swapped = core_swap(cat([x_one, y_one[3 * rows:]]))]
  transfers between devices with their start and end apart: 2 -> 15, of which waited for: 1 -> 7; matrix products, arithmetic and copies ran while one was open for 0% -> 7% of each run, Pallas kernels for 0% -> 2%
where the time goes in v1:
time: 141 us; the launch traced here: 140 us
  starting transfers between devices  70.9 us (50%)
  waiting for transfers between devices  38.9 us (28%)
  Pallas kernels  13.4 us (10%)
  local copies, waits for them, and re-layouts  9.41 us (7%)
  other arithmetic  7.08 us (5%)
    ppermute x15, starting transfers between devices, swap(): return lax.ppermute(value, ('row', 'col'), pairs(partner))  70.9 us
    ppermute x15, waiting for transfers between devices, swap(): return lax.ppermute(value, ('row', 'col'), pairs(partner))  38.9 us
    pallas_call x1, Pallas kernels, multiply_parts(): pl.pallas_call(kernel, out_shape=jax.ShapeDtypeStruct((band * BLK, slab *...  10.3 us
    unnamed x28, local copies, waits for them, and re-layouts  4.66 us
    pallas_call x2, Pallas kernels, hold(): pl.pallas_call(kernel, out_shape=jax.ShapeDtypeStruct(value.shape, value....  3.16 us
  transfers between devices with their start and end apart: 15, of which 7 were waited for; matrix products, arithmetic and copies ran while one was open for 7% of the time, Pallas kernels for 2%

profile of v1, /device:TPU:1, one launch (start us, length us, event | category | flops | bytes accessed | tf_op | source)
XLA Modules:
  0.0 140.0 jit_solution(8701419815611488953)
XLA Ops:
  0.0 1.6 %constant_dynamic-update-slice_fusion.21 = (bf16[2176,128]{1,0:T(8,128)(2,1)S(1)}, bf16[4352,128]{1,0:T(8,128)(2,1)}, bf16[2976,128]{1,0:T(8,128)(2,1)}) fusion(bf16[256,128]{1,0:T(8,128)(2,1)} %bitcast.14), kind=kLoop, calls=%fused_computation.32 | loop fusion | bytes 262144
  1.6 1.0 fusion.15
  4.1 9.6 %collective-permute-start.2 = (bf16[272,128]{1,0:T(8,128)(2,1)S(1)}, bf16[272,128]{1,0:T(8,128)(2,1)S(1)}, u32[]{:S(2)}, u32[]{:S(2)}) collective-permute-start(bf16[272,128]{1,0:T(8,128)(2,1)S(1)} %pad_maximum_fusion.7), channel_id=1, source_target_pairs={{0,512},{1,513},{2,514},{3,515},{4,516},{5,517},{6,518},{7,519},{8... | collective-permute-start | bytes 208904 | tf_op jit(solution)/shard_map/ppermute | solution.py:37
  13.7 0.9 constant_dynamic-update-slice_fusion.10
  16.1 0.9 pad_maximum_fusion.6
  17.0 8.3 %collective-permute-start = (bf16[400,128]{1,0:T(8,128)(2,1)S(1)}, bf16[400,128]{1,0:T(8,128)(2,1)S(1)}, u32[]{:S(2)}, u32[]{:S(2)}) collective-permute-start(bf16[400,128]{1,0:T(8,128)(2,1)S(1)} %pad_maximum_fusion.6), channel_id=1, source_target_pairs={{0,16},{1,17},{2,18},{3,19},{4,20},{5,21},{6,22},{7,23},{8,24},{9,... | collective-permute-start | bytes 307208 | tf_op jit(solution)/shard_map/ppermute | solution.py:37
  26.2 1.9 %collective-permute-start.3 = (bf16[544,128]{1,0:T(8,128)(2,1)S(1)}, bf16[544,128]{1,0:T(8,128)(2,1)S(1)}, u32[]{:S(2)}, u32[]{:S(2)}) collective-permute-start(bf16[544,128]{1,0:T(8,128)(2,1)S(1)} %pad_maximum_fusion.5), channel_id=1, source_target_pairs={{0,256},{1,257},{2,258},{3,259},{4,260},{5,261},{6,262},{7,263},{8... | collective-permute-start | bytes 417800 | tf_op jit(solution)/shard_map/ppermute | solution.py:37
  28.8 16.2 %collective-permute-start.1 = (bf16[800,128]{1,0:T(8,128)(2,1)S(1)}, bf16[800,128]{1,0:T(8,128)(2,1)S(1)}, u32[]{:S(2)}, u32[]{:S(2)}) collective-permute-start(bf16[800,128]{1,0:T(8,128)(2,1)S(1)} %pad_maximum_fusion.4), channel_id=1, source_target_pairs={{0,1},{1,0},{2,3},{3,2},{4,5},{5,4},{6,7},{7,6},{8,9},{9,8},{10,11... | collective-permute-start | bytes 614408 | tf_op jit(solution)/shard_map/ppermute | solution.py:37
  45.1 1.9 %collective-permute-start.4 = (bf16[1088,128]{1,0:T(8,128)(2,1)S(1)}, bf16[1088,128]{1,0:T(8,128)(2,1)S(1)}, u32[]{:S(2)}, u32[]{:S(2)}) collective-permute-start(bf16[1088,128]{1,0:T(8,128)(2,1)S(1)} %pad_maximum_fusion.3), channel_id=1, source_target_pairs={{0,128},{1,129},{2,130},{3,131},{4,132},{5,133},{6,134},{7,135},{8... | collective-permute-start | bytes 835592 | tf_op jit(solution)/shard_map/ppermute | solution.py:37
  47.8 5.7 %collective-permute-done.1 = bf16[800,128]{1,0:T(8,128)(2,1)S(1)} collective-permute-done((bf16[800,128]{1,0:T(8,128)(2,1)S(1)}, bf16[800,128]{1,0:T(8,128)(2,1)S(1)}, u32[]{:S(2)}, u32[]{:S(2)}) %collective-permute-start.1) | collective-permute-done | bytes 204832 | tf_op jit(solution)/shard_map/ppermute | solution.py:37
  54.1 1.6 %hold.2 = bf16[400,128]{1,0:T(8,128)(2,1)} custom-call(bf16[400,128]{1,0:T(8,128)(2,1)} %slice.64.in_ref), custom_call_target="tpu_custom_call" | custom-call | flops 99999997952 | tf_op jit(solution)/shard_map/hold/pallas_call | solution.py:68
  55.8 13.0 %collective-permute-done.4 = bf16[1088,128]{1,0:T(8,128)(2,1)S(1)} collective-permute-done((bf16[1088,128]{1,0:T(8,128)(2,1)S(1)}, bf16[1088,128]{1,0:T(8,128)(2,1)S(1)}, u32[]{:S(2)}, u32[]{:S(2)}) %collective-permute-start.4) | collective-permute-done | bytes 278560 | tf_op jit(solution)/shard_map/ppermute | solution.py:37
  69.6 1.9 %collective-permute-start.5 = (bf16[2976,128]{1,0:T(8,128)(2,1)S(1)}, bf16[2976,128]{1,0:T(8,128)(2,1)S(1)}, u32[]{:S(2)}, u32[]{:S(2)}) collective-permute-start(bf16[2976,128]{1,0:T(8,128)(2,1)S(1)} %slice_dynamic-update-slice_fusion.2), channel_id=1, source_target_pairs={{0,16},{1,17},{2,18},{3,19},{4,20},{5,21},{6,22},{7,23},{8,24},{9,... | collective-permute-start | bytes 2285576 | tf_op jit(solution)/shard_map/ppermute | solution.py:37
  71.5 2.2 %collective-permute-done.5 = bf16[2976,128]{1,0:T(8,128)(2,1)S(1)} collective-permute-done((bf16[2976,128]{1,0:T(8,128)(2,1)S(1)}, bf16[2976,128]{1,0:T(8,128)(2,1)S(1)}, u32[]{:S(2)}, u32[]{:S(2)}) %collective-permute-start.5) | collective-permute-done | bytes 761888 | tf_op jit(solution)/shard_map/ppermute | solution.py:37
  74.6 3.2 %collective-permute-start.7 = (bf16[4352,128]{1,0:T(8,128)(2,1)}, bf16[4352,128]{1,0:T(8,128)(2,1)S(1)}, u32[]{:S(2)}, u32[]{:S(2)}) collective-permute-start(bf16[4352,128]{1,0:T(8,128)(2,1)} %get-tuple-element.12), channel_id=1, source_target_pairs={{0,32},{1,33},{2,34},{3,35},{4,36},{5,37},{6,38},{7,39},{8,40},{9,... | collective-permute-start | bytes 3342344 | tf_op jit(solution)/shard_map/ppermute | solution.py:37
  77.9 4.6 %collective-permute-start.6 = (bf16[2400,128]{1,0:T(8,128)(2,1)S(1)}, bf16[2400,128]{1,0:T(8,128)(2,1)S(1)}, u32[]{:S(2)}, u32[]{:S(2)}) collective-permute-start(bf16[2400,128]{1,0:T(8,128)(2,1)S(1)} %get-tuple-element.13), channel_id=1, source_target_pairs={{0,4},{1,5},{2,6},{3,7},{4,0},{5,1},{6,2},{7,3},{8,12},{9,13},{10,... | collective-permute-start | bytes 1843208 | tf_op jit(solution)/shard_map/ppermute | solution.py:37
  82.6 7.9 %collective-permute-start.9 = (bf16[400,128]{1,0:T(8,128)(2,1)S(1)}, bf16[400,128]{1,0:T(8,128)(2,1)S(1)}, u32[]{:S(2)}, u32[]{:S(2)}) collective-permute-start(bf16[400,128]{1,0:T(8,128)(2,1)S(1)} %copy-done.5), channel_id=1, source_target_pairs={{0,3},{1,2},{2,1},{3,0},{4,7},{5,6},{6,5},{7,4},{8,11},{9,10},{10,... | collective-permute-start | bytes 307208 | tf_op jit(solution)/shard_map/ppermute | solution.py:37
  90.6 2.0 %collective-permute-done.7.refs_11_ = bf16[4352,128]{1,0:T(8,128)(2,1)S(1)} collective-permute-done((bf16[4352,128]{1,0:T(8,128)(2,1)}, bf16[4352,128]{1,0:T(8,128)(2,1)S(1)}, u32[]{:S(2)}, u32[]{:S(2)}) %collective-permute-start.7) | collective-permute-done | bytes 1114144 | tf_op jit(solution)/shard_map/ppermute | solution.py:37
  92.6 1.2 pad_maximum_fusion
  93.8 1.9 %collective-permute-start.11 = (bf16[5552,128]{1,0:T(8,128)(2,1)}, bf16[5552,128]{1,0:T(8,128)(2,1)}, u32[]{:S(2)}, u32[]{:S(2)}) collective-permute-start(bf16[5552,128]{1,0:T(8,128)(2,1)} %pad_maximum_fusion), channel_id=1, source_target_pairs={{0,16},{1,17},{2,18},{3,19},{4,20},{5,21},{6,22},{7,23},{8,24},{9,... | collective-permute-start | bytes 4263944 | tf_op jit(solution)/shard_map/ppermute | solution.py:37
  95.7 6.3 %collective-permute-done.9.in_ref = bf16[400,128]{1,0:T(8,128)(2,1)S(1)} collective-permute-done((bf16[400,128]{1,0:T(8,128)(2,1)S(1)}, bf16[400,128]{1,0:T(8,128)(2,1)S(1)}, u32[]{:S(2)}, u32[]{:S(2)}) %collective-permute-start.9) | collective-permute-done | bytes 102432 | tf_op jit(solution)/shard_map/ppermute | solution.py:37
  102.7 1.5 %hold.3.refs_6_ = bf16[400,128]{1,0:T(8,128)(2,1)} custom-call(bf16[400,128]{1,0:T(8,128)(2,1)} %copy-done.9), custom_call_target="tpu_custom_call" | custom-call | flops 99999997952 | tf_op jit(solution)/shard_map/hold/pallas_call | solution.py:68
  104.3 2.3 %collective-permute-start.8 = (bf16[2176,128]{1,0:T(8,128)(2,1)S(1)}, bf16[2176,128]{1,0:T(8,128)(2,1)S(1)}, u32[]{:S(2)}, u32[]{:S(2)}) collective-permute-start(bf16[2176,128]{1,0:T(8,128)(2,1)S(1)} %slice.70), channel_id=1, source_target_pairs={{0,96},{1,97},{2,98},{3,99},{4,100},{5,101},{6,102},{7,103},{8,104... | collective-permute-start | bytes 1671176 | tf_op jit(solution)/shard_map/ppermute | solution.py:37
  106.6 1.9 %collective-permute-start.10 = (bf16[1600,128]{1,0:T(8,128)(2,1)S(1)}, bf16[1600,128]{1,0:T(8,128)(2,1)S(1)}, u32[]{:S(2)}, u32[]{:S(2)}) collective-permute-start(bf16[1600,128]{1,0:T(8,128)(2,1)S(1)} %pad_maximum_fusion.1), channel_id=1, source_target_pairs={{0,12},{1,13},{2,14},{3,15},{4,8},{5,9},{6,10},{7,11},{8,4},{9,5},... | collective-permute-start | bytes 1228808 | tf_op jit(solution)/shard_map/ppermute | solution.py:37
  108.5 7.0 %collective-permute-done.10.refs_4_ = bf16[1600,128]{1,0:T(8,128)(2,1)S(1)} collective-permute-done((bf16[1600,128]{1,0:T(8,128)(2,1)S(1)}, bf16[1600,128]{1,0:T(8,128)(2,1)S(1)}, u32[]{:S(2)}, u32[]{:S(2)}) %collective-permute-start.10) | collective-permute-done | bytes 409632 | tf_op jit(solution)/shard_map/ppermute | solution.py:37
  115.6 2.3 %collective-permute-start.14 = (bf16[2176,128]{1,0:T(8,128)(2,1)S(1)}, bf16[2176,128]{1,0:T(8,128)(2,1)S(1)}, u32[]{:S(2)}, u32[]{:S(2)}) collective-permute-start(bf16[2176,128]{1,0:T(8,128)(2,1)S(1)} %collective-permute-done.8.refs_13_), channel_id=1, source_target_pairs={{0,16},{1,17},{2,18},{3,19},{4,20},{5,21},{6,22},{7,23},{8,24},{9,... | collective-permute-start | bytes 1671176 | tf_op jit(solution)/shard_map/ppermute | solution.py:37
  118.0 4.8 %collective-permute-start.12 = (bf16[400,128]{1,0:T(8,128)(2,1)S(1)}, bf16[400,128]{1,0:T(8,128)(2,1)S(1)}, u32[]{:S(2)}, u32[]{:S(2)}) collective-permute-start(bf16[400,128]{1,0:T(8,128)(2,1)S(1)} %copy-done), channel_id=1, source_target_pairs={{0,4},{1,5},{2,6},{3,7},{4,0},{5,1},{6,2},{7,3},{8,12},{9,13},{10,... | collective-permute-start | bytes 307208 | tf_op jit(solution)/shard_map/ppermute | solution.py:37
  122.8 1.9 %collective-permute-start.13 = (bf16[400,128]{1,0:T(8,128)(2,1)S(1)}, bf16[400,128]{1,0:T(8,128)(2,1)S(1)}, u32[]{:S(2)}, u32[]{:S(2)}) collective-permute-start(bf16[400,128]{1,0:T(8,128)(2,1)S(1)} %copy-done), channel_id=1, source_target_pairs={{0,8},{1,9},{2,10},{3,11},{4,12},{5,13},{6,14},{7,15},{8,0},{9,1},... | collective-permute-start | bytes 307208 | tf_op jit(solution)/shard_map/ppermute | solution.py:37
  124.8 1.3 slice.73.refs_12_
  126.1 1.0 slice.72.refs_5_
  127.1 2.6 %collective-permute-done.13.refs_8_ = bf16[400,128]{1,0:T(8,128)(2,1)S(1)} collective-permute-done((bf16[400,128]{1,0:T(8,128)(2,1)S(1)}, bf16[400,128]{1,0:T(8,128)(2,1)S(1)}, u32[]{:S(2)}, u32[]{:S(2)}) %collective-permute-start.13) | collective-permute-done | bytes 102432 | tf_op jit(solution)/shard_map/ppermute | solution.py:37
  129.7 10.3 %block_products.1 = bf16[256,1024]{1,0:T(8,128)(2,1)} custom-call(s32[2]{0:T(128)S(1)} %pad_add_fusion.refs_0_, s32[2,8]{1,0:T(2,128)S(1)} %copy-done.1, bf16[1200,128]{1,0:T(8,128)(2,1)S(1)} %pad_maximum_fusion.2.refs_2_, bf16[1200,128]{1,0:T(8,128)(2,1)S(1)} %get-tuple-element.16.refs_3_, bf16[1600,128]{1,0:T(8,128)(2,1)S(1)} %collective-permute-done.10.refs_4_, ...), custom_call_target="tpu_custom_call" | custom-call | tf_op jit(solution)/shard_map/block_products/pallas_call | solution.py:230
  (53 shorter events, 8.6 us)
Async XLA Ops:
  0.0 45.0 %copy-start.4 = (bf16[2,128,128]{2,1,0:T(8,128)(2,1)S(1)}, bf16[2,128,128]{2,1,0:T(8,128)(2,1)}, u32[]{:S(2)}) copy-start(bf16[2,128,128]{2,1,0:T(8,128)(2,1)} %param.7) | copy-start | bytes 196612
  0.0 28.8 %copy-start.2 = (bf16[3,128,128]{2,1,0:T(8,128)(2,1)S(1)}, bf16[3,128,128]{2,1,0:T(8,128)(2,1)}, u32[]{:S(2)}) copy-start(bf16[3,128,128]{2,1,0:T(8,128)(2,1)} %param.5) | copy-start | bytes 294916
  4.1 21.2 %collective-permute-start.2 = (bf16[272,128]{1,0:T(8,128)(2,1)S(1)}, bf16[272,128]{1,0:T(8,128)(2,1)S(1)}, u32[]{:S(2)}, u32[]{:S(2)}) collective-permute-start(bf16[272,128]{1,0:T(8,128)(2,1)S(1)} %pad_maximum_fusion.7), channel_id=1, source_target_pairs={{0,512},{1,513},{2,514},{3,515},{4,516},{5,517},{6,518},{7,519},{8... | collective-permute-start | bytes 208904 | tf_op jit(solution)/shard_map/ppermute | solution.py:37
  16.1 28.9 %copy-start.6 = (bf16[16,128]{1,0:T(8,128)(2,1)}, bf16[16,128]{1,0:T(8,128)(2,1)S(1)}, u32[]{:S(2)}) copy-start(bf16[16,128]{1,0:T(8,128)(2,1)S(1)} %get-tuple-element.36) | copy-start | bytes 12292
  17.0 11.8 %collective-permute-start = (bf16[400,128]{1,0:T(8,128)(2,1)S(1)}, bf16[400,128]{1,0:T(8,128)(2,1)S(1)}, u32[]{:S(2)}, u32[]{:S(2)}) collective-permute-start(bf16[400,128]{1,0:T(8,128)(2,1)S(1)} %pad_maximum_fusion.6), channel_id=1, source_target_pairs={{0,16},{1,17},{2,18},{3,19},{4,20},{5,21},{6,22},{7,23},{8,24},{9,... | collective-permute-start | bytes 307208 | tf_op jit(solution)/shard_map/ppermute | solution.py:37
  26.2 18.8 %collective-permute-start.3 = (bf16[544,128]{1,0:T(8,128)(2,1)S(1)}, bf16[544,128]{1,0:T(8,128)(2,1)S(1)}, u32[]{:S(2)}, u32[]{:S(2)}) collective-permute-start(bf16[544,128]{1,0:T(8,128)(2,1)S(1)} %pad_maximum_fusion.5), channel_id=1, source_target_pairs={{0,256},{1,257},{2,258},{3,259},{4,260},{5,261},{6,262},{7,263},{8... | collective-permute-start | bytes 417800 | tf_op jit(solution)/shard_map/ppermute | solution.py:37
  28.8 24.7 %collective-permute-start.1 = (bf16[800,128]{1,0:T(8,128)(2,1)S(1)}, bf16[800,128]{1,0:T(8,128)(2,1)S(1)}, u32[]{:S(2)}, u32[]{:S(2)}) collective-permute-start(bf16[800,128]{1,0:T(8,128)(2,1)S(1)} %pad_maximum_fusion.4), channel_id=1, source_target_pairs={{0,1},{1,0},{2,3},{3,2},{4,5},{5,4},{6,7},{7,6},{8,9},{9,8},{10,11... | collective-permute-start | bytes 614408 | tf_op jit(solution)/shard_map/ppermute | solution.py:37
  45.1 23.7 %collective-permute-start.4 = (bf16[1088,128]{1,0:T(8,128)(2,1)S(1)}, bf16[1088,128]{1,0:T(8,128)(2,1)S(1)}, u32[]{:S(2)}, u32[]{:S(2)}) collective-permute-start(bf16[1088,128]{1,0:T(8,128)(2,1)S(1)} %pad_maximum_fusion.3), channel_id=1, source_target_pairs={{0,128},{1,129},{2,130},{3,131},{4,132},{5,133},{6,134},{7,135},{8... | collective-permute-start | bytes 835592 | tf_op jit(solution)/shard_map/ppermute | solution.py:37
  54.1 14.6 %copy-start.8 = (bf16[2976,128]{1,0:T(8,128)(2,1)S(1)}, bf16[2976,128]{1,0:T(8,128)(2,1)}, u32[]{:S(2)}) copy-start(bf16[2976,128]{1,0:T(8,128)(2,1)} %get-tuple-element.22) | copy-start | bytes 2285572
  55.8 13.8 %copy-start.5 = (bf16[400,128]{1,0:T(8,128)(2,1)S(1)}, bf16[400,128]{1,0:T(8,128)(2,1)}, u32[]{:S(2)}) copy-start(bf16[400,128]{1,0:T(8,128)(2,1)} %hold.2) | copy-start | bytes 307204
  69.6 4.1 %collective-permute-start.5 = (bf16[2976,128]{1,0:T(8,128)(2,1)S(1)}, bf16[2976,128]{1,0:T(8,128)(2,1)S(1)}, u32[]{:S(2)}, u32[]{:S(2)}) collective-permute-start(bf16[2976,128]{1,0:T(8,128)(2,1)S(1)} %slice_dynamic-update-slice_fusion.2), channel_id=1, source_target_pairs={{0,16},{1,17},{2,18},{3,19},{4,20},{5,21},{6,22},{7,23},{8,24},{9,... | collective-permute-start | bytes 2285576 | tf_op jit(solution)/shard_map/ppermute | solution.py:37
  74.6 17.9 %collective-permute-start.7 = (bf16[4352,128]{1,0:T(8,128)(2,1)}, bf16[4352,128]{1,0:T(8,128)(2,1)S(1)}, u32[]{:S(2)}, u32[]{:S(2)}) collective-permute-start(bf16[4352,128]{1,0:T(8,128)(2,1)} %get-tuple-element.12), channel_id=1, source_target_pairs={{0,32},{1,33},{2,34},{3,35},{4,36},{5,37},{6,38},{7,39},{8,40},{9,... | collective-permute-start | bytes 3342344 | tf_op jit(solution)/shard_map/ppermute | solution.py:37
  77.9 12.6 %collective-permute-start.6 = (bf16[2400,128]{1,0:T(8,128)(2,1)S(1)}, bf16[2400,128]{1,0:T(8,128)(2,1)S(1)}, u32[]{:S(2)}, u32[]{:S(2)}) collective-permute-start(bf16[2400,128]{1,0:T(8,128)(2,1)S(1)} %get-tuple-element.13), channel_id=1, source_target_pairs={{0,4},{1,5},{2,6},{3,7},{4,0},{5,1},{6,2},{7,3},{8,12},{9,13},{10,... | collective-permute-start | bytes 1843208 | tf_op jit(solution)/shard_map/ppermute | solution.py:37
  82.6 19.5 %collective-permute-start.9 = (bf16[400,128]{1,0:T(8,128)(2,1)S(1)}, bf16[400,128]{1,0:T(8,128)(2,1)S(1)}, u32[]{:S(2)}, u32[]{:S(2)}) collective-permute-start(bf16[400,128]{1,0:T(8,128)(2,1)S(1)} %copy-done.5), channel_id=1, source_target_pairs={{0,3},{1,2},{2,1},{3,0},{4,7},{5,6},{6,5},{7,4},{8,11},{9,10},{10,... | collective-permute-start | bytes 307208 | tf_op jit(solution)/shard_map/ppermute | solution.py:37
  93.8 31.0 %collective-permute-start.11 = (bf16[5552,128]{1,0:T(8,128)(2,1)}, bf16[5552,128]{1,0:T(8,128)(2,1)}, u32[]{:S(2)}, u32[]{:S(2)}) collective-permute-start(bf16[5552,128]{1,0:T(8,128)(2,1)} %pad_maximum_fusion), channel_id=1, source_target_pairs={{0,16},{1,17},{2,18},{3,19},{4,20},{5,21},{6,22},{7,23},{8,24},{9,... | collective-permute-start | bytes 4263944 | tf_op jit(solution)/shard_map/ppermute | solution.py:37
  102.1 0.6 copy-start.9
  104.2 2.3 %copy-start = (bf16[400,128]{1,0:T(8,128)(2,1)S(1)}, bf16[400,128]{1,0:T(8,128)(2,1)}, u32[]{:S(2)}) copy-start(bf16[400,128]{1,0:T(8,128)(2,1)} %hold.3.refs_6_) | copy-start | bytes 307204
  104.2 20.5 %copy-start.3 = (bf16[3,128,128]{2,1,0:T(8,128)(2,1)S(1)}, bf16[3,128,128]{2,1,0:T(8,128)(2,1)}, u32[]{:S(2)}) copy-start(bf16[3,128,128]{2,1,0:T(8,128)(2,1)} %param.5) | copy-start | bytes 294916
  104.2 20.5 %copy-start.7 = (bf16[16,128]{1,0:T(8,128)(2,1)S(1)}, bf16[16,128]{1,0:T(8,128)(2,1)}, u32[]{:S(2)}) copy-start(bf16[16,128]{1,0:T(8,128)(2,1)} %copy-done.6) | copy-start | bytes 12292
  104.3 11.3 %collective-permute-start.8 = (bf16[2176,128]{1,0:T(8,128)(2,1)S(1)}, bf16[2176,128]{1,0:T(8,128)(2,1)S(1)}, u32[]{:S(2)}, u32[]{:S(2)}) collective-permute-start(bf16[2176,128]{1,0:T(8,128)(2,1)S(1)} %slice.70), channel_id=1, source_target_pairs={{0,96},{1,97},{2,98},{3,99},{4,100},{5,101},{6,102},{7,103},{8,104... | collective-permute-start | bytes 1671176 | tf_op jit(solution)/shard_map/ppermute | solution.py:37
  106.6 9.0 %collective-permute-start.10 = (bf16[1600,128]{1,0:T(8,128)(2,1)S(1)}, bf16[1600,128]{1,0:T(8,128)(2,1)S(1)}, u32[]{:S(2)}, u32[]{:S(2)}) collective-permute-start(bf16[1600,128]{1,0:T(8,128)(2,1)S(1)} %pad_maximum_fusion.1), channel_id=1, source_target_pairs={{0,12},{1,13},{2,14},{3,15},{4,8},{5,9},{6,10},{7,11},{8,4},{9,5},... | collective-permute-start | bytes 1228808 | tf_op jit(solution)/shard_map/ppermute | solution.py:37
  115.6 14.1 %collective-permute-start.14 = (bf16[2176,128]{1,0:T(8,128)(2,1)S(1)}, bf16[2176,128]{1,0:T(8,128)(2,1)S(1)}, u32[]{:S(2)}, u32[]{:S(2)}) collective-permute-start(bf16[2176,128]{1,0:T(8,128)(2,1)S(1)} %collective-permute-done.8.refs_13_), channel_id=1, source_target_pairs={{0,16},{1,17},{2,18},{3,19},{4,20},{5,21},{6,22},{7,23},{8,24},{9,... | collective-permute-start | bytes 1671176 | tf_op jit(solution)/shard_map/ppermute | solution.py:37
  118.0 9.2 %collective-permute-start.12 = (bf16[400,128]{1,0:T(8,128)(2,1)S(1)}, bf16[400,128]{1,0:T(8,128)(2,1)S(1)}, u32[]{:S(2)}, u32[]{:S(2)}) collective-permute-start(bf16[400,128]{1,0:T(8,128)(2,1)S(1)} %copy-done), channel_id=1, source_target_pairs={{0,4},{1,5},{2,6},{3,7},{4,0},{5,1},{6,2},{7,3},{8,12},{9,13},{10,... | collective-permute-start | bytes 307208 | tf_op jit(solution)/shard_map/ppermute | solution.py:37
  122.8 6.9 %collective-permute-start.13 = (bf16[400,128]{1,0:T(8,128)(2,1)S(1)}, bf16[400,128]{1,0:T(8,128)(2,1)S(1)}, u32[]{:S(2)}, u32[]{:S(2)}) collective-permute-start(bf16[400,128]{1,0:T(8,128)(2,1)S(1)} %copy-done), channel_id=1, source_target_pairs={{0,8},{1,9},{2,10},{3,11},{4,12},{5,13},{6,14},{7,15},{8,0},{9,1},... | collective-permute-start | bytes 307208 | tf_op jit(solution)/shard_map/ppermute | solution.py:37
  124.8 4.9 %copy-start.1 = (s32[2,8]{1,0:T(2,128)S(1)}, s32[2,8]{1,0:T(2,128)}, u32[]{:S(2)}) copy-start(s32[2,8]{1,0:T(2,128)} %refs_1_.1) | copy-start | bytes 196

commit v2 on v1

v2 whole, which is shorter than its diff:
```python
import jax
import jax.numpy as jnp
from jax import lax
from jax.experimental import pallas as pl
from jax.experimental.pallas import tpu as pltpu
from jax.sharding import PartitionSpec as P

Z_LO, X, CORE, Y, Z_HI = 8, 4, 2, 4, 4
BLK = 128
HOLD = 10**11
GROUP = 4
META = 16
A_SLOTS, B_SLOTS = 3, 2
A_ROWS = A_SLOTS * BLK + META
B_ROWS = B_SLOTS * BLK + META
K_COL = 72
K_ROW = 18


def pairs(partner):
    out = []
    for zl in range(Z_LO):
        for x in range(X):
            for q in range(CORE):
                for y in range(Y):
                    for zh in range(Z_HI):
                        a, b, c, d, e = partner(zl, x, q, y, zh)
                        out.append(
                            (
                                (((zl * X + x) * CORE + q) * Y + y) * Z_HI + zh,
                                (((a * X + b) * CORE + c) * Y + d) * Z_HI + e,
                            )
                        )
    return out


def swap(value, partner):
    return lax.ppermute(value, ("row", "col"), pairs(partner))


def z_lo_swap(value, d):
    return swap(value, lambda zl, x, q, y, zh: (zl ^ d, x, q, y, zh))


def z_hi_swap(value, first, second):
    return swap(value, lambda zl, x, q, y, zh: (zl, x, q, y, zh ^ (second if q else first)))


def y_swap(value, first, second):
    return swap(value, lambda zl, x, q, y, zh: (zl, x, q, y ^ (second if q else first), zh))


def x_swap(value, first, second):
    return swap(value, lambda zl, x, q, y, zh: (zl, x ^ (second if q else first), q, y, zh))


def core_swap(value):
    return swap(value, lambda zl, x, q, y, zh: (zl, x, q ^ 1, y, zh))


def after(value, *others):
    return lax.optimization_barrier((value, *others))[0]


def hold(value, flops):
    def kernel(in_ref, out_ref):
        out_ref[...] = in_ref[...]

    head = pl.pallas_call(
        kernel,
        out_shape=jax.ShapeDtypeStruct((META, value.shape[1]), value.dtype),
        cost_estimate=pl.CostEstimate(flops=flops, bytes_accessed=0, transcendentals=0),
        name="hold",
    )(value[:META])
    return jnp.concatenate([head, value[META:]])


def pack_kernel(left_index, right_index, left_blocks, right_blocks, left_out, right_out, sems):
    copies = []
    for blocks, out in ((left_blocks, left_out), (right_blocks, right_out)):
        for s in range(blocks.shape[0]):
            copy = pltpu.make_async_copy(
                blocks.at[s], out.at[pl.ds(s * BLK, BLK)], sems.at[len(copies)]
            )
            copy.start()
            copies.append(copy)
    lane = lax.broadcasted_iota(jnp.int32, (META, BLK), 1)

    def write(out, values):
        meta = jnp.zeros((META, BLK), jnp.int32)
        for n, value in enumerate(values):
            meta = jnp.where(lane == n, value, meta)
        out[pl.ds(out.shape[0] - META, META), :] = meta.astype(jnp.float32).astype(jnp.bfloat16)

    row, col = lax.axis_index("row"), lax.axis_index("col")
    columns = [left_index[s, 1] for s in range(A_SLOTS)]
    offsets = [jnp.where(k >= 0, k - col * K_COL, -1) for k in columns]
    bands = [jnp.clip(left_index[s, 0], 0, 1) for s in range(A_SLOTS)]
    write(left_out, offsets + bands)
    offsets = [right_index[s, 0] - row * K_ROW for s in range(B_SLOTS)]
    live = [o < K_ROW for o in offsets]
    offsets = [jnp.where(f, o, -1) for f, o in zip(live, offsets)]
    write(right_out, offsets + [jnp.where(live[s], right_index[s, 1], 0) for s in range(B_SLOTS)])
    for copy in copies:
        copy.wait()


def pack(left_index, right_index, left_blocks, right_blocks):
    smem = pl.BlockSpec(memory_space=pltpu.SMEM)
    anywhere = pl.BlockSpec(memory_space=pl.ANY)
    vmem = pl.BlockSpec(memory_space=pltpu.VMEM)
    return pl.pallas_call(
        pack_kernel,
        out_shape=[
            jax.ShapeDtypeStruct((A_ROWS, BLK), jnp.bfloat16),
            jax.ShapeDtypeStruct((B_ROWS, BLK), jnp.bfloat16),
        ],
        in_specs=[smem, smem, anywhere, anywhere],
        out_specs=[vmem, vmem],
        scratch_shapes=[pltpu.SemaphoreType.DMA((A_SLOTS + B_SLOTS,))],
        compiler_params=pltpu.CompilerParams(vmem_limit_bytes=56 * 1024 * 1024),
        name="pack",
    )(left_index, right_index, left_blocks, right_blocks)


def gather(left, right):
    rows = A_ROWS
    cat = jnp.concatenate
    sibling = core_swap(left)
    right = cat([right, z_lo_swap(right, 4)])
    z_one = z_hi_swap(cat([left, sibling]), 1, 3)
    right = cat([right, z_lo_swap(right, 2)])
    z_one_mine = hold(z_one[:rows], HOLD)
    right = cat([right, z_lo_swap(right, 1)])
    high = right.shape[0]
    z_two = z_hi_swap(z_one[:rows], 3, 1)
    swapped = core_swap(cat([right, z_one_mine, z_one[rows:]]))
    near_right, z_other = swapped[:high], swapped[high:]
    x_one = x_swap(cat([right, near_right]), 1, 3)
    mine = cat([left, z_one_mine, z_other[rows:]])
    others = cat([sibling, z_one[rows:], z_other[:rows]])
    others, z_two = lax.optimization_barrier((others, z_two))
    y_one = y_swap(cat([mine, others]), 1, 3)
    z_near = y_swap(z_two, 1, 3)
    x_one, y_one, z_near = lax.optimization_barrier((x_one, y_one, z_near))
    x_two = x_swap(x_one[:high], 3, 1)
    y_two = y_swap(cat([y_one[: 3 * rows], z_two, z_near]), 3, 1)
    swapped = core_swap(cat([x_one, y_one[3 * rows :]]))
    x_last = core_swap(x_two)
    return (
        [mine, y_one[: 3 * rows], y_two, swapped[2 * high :], z_two, z_near],
        [right, near_right, x_one, swapped[: 2 * high], x_two, x_last],
    )


def product_kernel(n_left, n_right, pattern_ref, *refs):
    left_parts = refs[:n_left]
    right_parts = refs[n_left : n_left + n_right]
    out_ref = refs[n_left + n_right]
    (
        left,
        right,
        total,
        left_raw,
        right_raw,
        left_meta,
        right_meta,
        left_keys,
        right_keys,
        work,
        sems,
        raw_sems,
        key_sems,
    ) = refs[n_left + n_right + 1 :]
    raw_copies, copies = [], []
    for parts, raw, rows in ((left_parts, left_raw, A_ROWS), (right_parts, right_raw, B_ROWS)):
        at = 0
        for part in parts:
            n = part.shape[0]
            copy = pltpu.make_async_copy(
                part.at[:, pl.ds(rows - META, META), :],
                raw.at[pl.ds(at, n)],
                raw_sems.at[len(raw_copies)],
            )
            copy.start()
            raw_copies.append(copy)
            at += n
    for parts, held in ((left_parts, left), (right_parts, right)):
        at = 0
        for part in parts:
            n = part.shape[0]
            copy = pltpu.make_async_copy(part, held.at[pl.ds(at, n)], sems.at[len(copies)])
            copy.start()
            copies.append(copy)
            at += n
    total[...] = jnp.zeros_like(total)
    for copy in raw_copies:
        copy.wait()
    n_a, n_b = left_meta.shape[0], right_meta.shape[0]
    for i in range(n_a):
        left_meta[pl.ds(i, 1), :] = left_raw[i].astype(jnp.float32)[0:1].astype(jnp.int32)
    for i in range(n_b):
        right_meta[pl.ds(i, 1), :] = right_raw[i].astype(jnp.float32)[0:1].astype(jnp.int32)
    right_copy = pltpu.make_async_copy(right_meta, right_keys, key_sems.at[1])
    right_copy.start()

    row, col = lax.axis_index("row"), lax.axis_index("col")
    zl, x, q = row // (X * CORE), (row // CORE) % X, row % CORE
    y, zh = col // Z_HI, col % Z_HI
    near, far = jnp.where(q == 0, 1, 3), jnp.where(q == 0, 3, 1)
    i = lax.broadcasted_iota(jnp.int32, left_meta.shape, 0)
    lane = lax.broadcasted_iota(jnp.int32, left_meta.shape, 1)
    first = i < 9
    n = jnp.where(first, i, i - 2)
    r = (n >= 3).astype(jnp.int32) + (n >= 6).astype(jnp.int32) + (n >= 9).astype(jnp.int32)
    p = n - 3 * r
    one = jnp.where(first, near, far)
    two = jnp.where(first, far, near)
    dz = jnp.where(p == 0, 0, jnp.where(p == 1, one, two))
    dy = jnp.where(r == 0, 0, jnp.where(r == 1, near, jnp.where(r == 2, 2, far)))
    opposite = (i == 9) | (i == 10) | (i > 13)
    dz = jnp.where(opposite, 2, dz)
    dy = jnp.where(
        opposite,
        jnp.where(i == 9, far, jnp.where(i == 10, 2, jnp.where(i == 14, 0, near))),
        dy,
    )
    there = ((y ^ dy) << 2) + (zh ^ dz)
    meta = left_meta[...]
    live = meta >= 0
    offset = jnp.maximum(meta, 0)
    group = jnp.zeros_like(offset)
    for bound in range(K_ROW, K_COL, K_ROW):
        group += (offset >= bound).astype(jnp.int32)
    want = jnp.where(live, offset - group * K_ROW, K_ROW)
    other = there * (K_COL // K_ROW) + group
    e = (other & 1) ^ q
    u = ((other >> 1) & 3) ^ x
    w = (other >> 3) ^ zl
    m = ((w & 1) << 2) | (w & 2) | (w >> 2)
    part = jnp.where(
        u == 0,
        e,
        jnp.where(u == 2, 6 + e, jnp.where(u == near, 2 + e, 5 - e)),
    )
    code = ((part * Z_LO + m) << 8) | want
    left_meta[...] = jnp.where(lane < A_SLOTS, code, meta)
    left_copy = pltpu.make_async_copy(left_meta, left_keys, key_sems.at[0])
    left_copy.start()
    right_copy.wait()
    left_copy.wait()
    slab = pattern_ref.shape[1]
    spare = pattern_ref.shape[0] * slab

    def shard(i, count):
        for s in range(A_SLOTS):
            found = left_keys[i, s]
            band = left_keys[i, A_SLOTS + s]
            t = found >> 8
            wanted = found & 255
            for j in range(B_SLOTS):
                column = right_keys[t, B_SLOTS + j]
                hit = (right_keys[t, j] == wanted) & (pattern_ref[band, column] > 0)
                work[0, count] = i * A_SLOTS + s
                work[1, count] = t * B_SLOTS + j
                work[2, count] = band * slab + column
                count = count + hit.astype(jnp.int32)
        return count

    count = lax.fori_loop(0, n_a, shard, jnp.int32(0))
    for n in range(GROUP):
        work[0, count + n] = 0
        work[1, count + n] = 0
        work[2, count + n] = spare
    for copy in copies:
        copy.wait()

    def multiply(g, carry):
        products = []
        for n in range(GROUP):
            a, b = work[0, g * GROUP + n], work[1, g * GROUP + n]
            a_shard = a // A_SLOTS
            a_at = pl.multiple_of((a - a_shard * A_SLOTS) * BLK, BLK)
            b_at = pl.multiple_of((b & 1) * BLK, BLK)
            products.append(
                jnp.dot(
                    left[a_shard, pl.ds(a_at, BLK), :],
                    right[b >> 1, pl.ds(b_at, BLK), :],
                    preferred_element_type=jnp.float32,
                )
            )
        for n in range(GROUP):
            total[work[2, g * GROUP + n]] += products[n]
        return carry

    lax.fori_loop(0, (count + GROUP - 1) // GROUP, multiply, 0)
    for b in range(pattern_ref.shape[0]):
        for j in range(slab):
            out_ref[b * BLK : (b + 1) * BLK, j * BLK : (j + 1) * BLK] = total[b * slab + j].astype(
                out_ref.dtype
            )


def multiply_parts(left_parts, right_parts, pattern):
    band, slab = pattern.shape
    left_parts = [p.reshape(-1, A_ROWS, BLK) for p in left_parts]
    right_parts = [p.reshape(-1, B_ROWS, BLK) for p in right_parts]
    n_a = sum(p.shape[0] for p in left_parts)
    n_b = sum(p.shape[0] for p in right_parts)
    n_parts = len(left_parts) + len(right_parts)
    smem = pl.BlockSpec(memory_space=pltpu.SMEM)
    anywhere = pl.BlockSpec(memory_space=pl.ANY)

    def kernel(*refs):
        product_kernel(len(left_parts), len(right_parts), *refs)

    return pl.pallas_call(
        kernel,
        out_shape=jax.ShapeDtypeStruct((band * BLK, slab * BLK), jnp.bfloat16),
        in_specs=[smem] + [anywhere] * n_parts,
        out_specs=pl.BlockSpec(memory_space=pltpu.VMEM),
        scratch_shapes=[
            pltpu.VMEM((n_a, A_ROWS, BLK), jnp.bfloat16),
            pltpu.VMEM((n_b, B_ROWS, BLK), jnp.bfloat16),
            pltpu.VMEM((band * slab + 1, BLK, BLK), jnp.float32),
            pltpu.VMEM((n_a, META, BLK), jnp.bfloat16),
            pltpu.VMEM((n_b, META, BLK), jnp.bfloat16),
            pltpu.VMEM((n_a, BLK), jnp.int32),
            pltpu.VMEM((n_b, BLK), jnp.int32),
            pltpu.SMEM((n_a, BLK), jnp.int32),
            pltpu.SMEM((n_b, BLK), jnp.int32),
            pltpu.SMEM((3, n_a * A_SLOTS * B_SLOTS + GROUP), jnp.int32),
            pltpu.SemaphoreType.DMA((n_parts,)),
            pltpu.SemaphoreType.DMA((n_parts,)),
            pltpu.SemaphoreType.DMA((2,)),
        ],
        compiler_params=pltpu.CompilerParams(vmem_limit_bytes=24 * 1024 * 1024),
        name="block_products",
    )(pattern, *left_parts, *right_parts)


def per_device(left_blocks, left_index, right_blocks, right_index, out_pattern):
    left, right = pack(left_index, right_index, left_blocks, right_blocks)
    return multiply_parts(*gather(left, right), out_pattern)


def solution(mesh):
    placed = (
        P("row", "col", None),
        P("row", "col"),
        P("row", "col", None),
        P("row", "col"),
        P("row", "col"),
    )
    return jax.shard_map(
        per_device, mesh=mesh, in_specs=placed, out_specs=P("row", "col"), check_vma=False
    )
```

time: 141 us -> 134 us (0.950)
  waiting for transfers between devices: 38.9 us -> 48.1 us
  starting transfers between devices: 70.9 us -> 64.9 us
  other arithmetic: 7.08 us -> 2.04 us
  Pallas kernels: 13.4 us -> 9.76 us
  local copies, waits for them, and re-layouts: 9.41 us -> 7.67 us
    ppermute x15 -> x14, waiting for transfers between devices: 38.9 us -> 48.1 us  [swap(): return lax.ppermute(value, ('row', 'col'), pairs(partner))]
    ppermute x15 -> x14, starting transfers between devices: 70.9 us -> 64.9 us  [swap(): return lax.ppermute(value, ('row', 'col'), pairs(partner))]
    pallas_call x1, Pallas kernels: 10.3 us -> 6.25 us  [multiply_parts(): pl.pallas_call(kernel, out_shape=jax.ShapeDtypeStruct((band * BLK, slab *...]
    concatenate x4 -> x3, other arithmetic: 2.46 us -> 0.1 us  [the longest x1 0.04 us: gather(): right = cat([right, z_lo_swap(right, 1)])]
    unnamed x28 -> x18, local copies, waits for them, and re-layouts: 4.66 us -> 6.66 us
    another operation x3 -> x0, other arithmetic: 1.73 us -> none
  transfers between devices with their start and end apart: 15 -> 14, of which waited for: 7 -> 7; matrix products, arithmetic and copies ran while one was open for 7% -> 5% of each run, Pallas kernels for 2% -> 1%
where the time goes in v2:
time: 134 us; the launch traced here: 133 us
  starting transfers between devices  64.9 us (48%)
  waiting for transfers between devices  48.1 us (36%)
  Pallas kernels  9.76 us (7%)
  local copies, waits for them, and re-layouts  7.67 us (6%)
  other arithmetic  2.04 us (2%)
    ppermute x14, starting transfers between devices, swap(): return lax.ppermute(value, ('row', 'col'), pairs(partner))  64.9 us
    ppermute x14, waiting for transfers between devices, swap(): return lax.ppermute(value, ('row', 'col'), pairs(partner))  48.1 us
    unnamed x18, local copies, waits for them, and re-layouts  6.66 us
    pallas_call x1, Pallas kernels, multiply_parts(): pl.pallas_call(kernel, out_shape=jax.ShapeDtypeStruct((band * BLK, slab *...  6.25 us
  transfers between devices with their start and end apart: 14, of which 7 were waited for; matrix products, arithmetic and copies ran while one was open for 5% of the time, Pallas kernels for 1%

profile of v2, /device:TPU:1, one launch (start us, length us, event | category | flops | bytes accessed | tf_op | source)
XLA Modules:
  0.0 132.8 jit_solution(15975679638341911153)
XLA Ops:
  0.0 1.3 %copy.6.left_index = s32[3,2]{1,0:T(4,128)} copy(s32[3,2]{0,1:T(2,128)} %param.6) | data formatting | bytes 48 | tf_op args[1]
  1.3 2.2 %pack.1 = (bf16[400,128]{1,0:T(8,128)(2,1)}, bf16[272,128]{1,0:T(8,128)(2,1)}) custom-call(s32[3,2]{1,0:T(4,128)} %copy.6.left_index, s32[2,2]{1,0:T(2,128)} %right_index.1, bf16[3,128,128]{2,1,0:T(8,128)(2,1)} %left_blocks.1, bf16[2,128,128]{2,1,0:T(8,128)(2,1)} %right_blocks.1), custom_call_target="tpu_custom_call" | custom-call | tf_op jit(solution)/shard_map/pack/pallas_call | solution.py:112
  3.6 16.2 %collective-permute-start = (bf16[400,128]{1,0:T(8,128)(2,1)}, bf16[400,128]{1,0:T(8,128)(2,1)S(1)}, u32[]{:S(2)}, u32[]{:S(2)}) collective-permute-start(bf16[400,128]{1,0:T(8,128)(2,1)} %get-tuple-element.12), channel_id=1, source_target_pairs={{0,16},{1,17},{2,18},{3,19},{4,20},{5,21},{6,22},{7,23},{8,24},{9,... | collective-permute-start | bytes 307208 | tf_op jit(solution)/shard_map/ppermute | solution.py:38
  19.8 1.9 %collective-permute-start.2 = (bf16[272,128]{1,0:T(8,128)(2,1)}, bf16[272,128]{1,0:T(8,128)(2,1)S(1)}, u32[]{:S(2)}, u32[]{:S(2)}) collective-permute-start(bf16[272,128]{1,0:T(8,128)(2,1)} %get-tuple-element.13), channel_id=1, source_target_pairs={{0,512},{1,513},{2,514},{3,515},{4,516},{5,517},{6,518},{7,519},{8... | collective-permute-start | bytes 208904 | tf_op jit(solution)/shard_map/ppermute | solution.py:38
  21.7 1.5 %constant_dynamic-update-slice_fusion.9 = (bf16[4352,128]{1,0:T(8,128)(2,1)}, bf16[2976,128]{1,0:T(8,128)(2,1)S(1)}) fusion(bf16[272,128]{1,0:T(8,128)(2,1)} %get-tuple-element.13), kind=kLoop, calls=%fused_computation.18 | loop fusion | bytes 208896
  23.3 0.9 constant_dynamic-update-slice_fusion.14
  24.2 5.4 %collective-permute-done.2 = bf16[272,128]{1,0:T(8,128)(2,1)S(1)} collective-permute-done((bf16[272,128]{1,0:T(8,128)(2,1)}, bf16[272,128]{1,0:T(8,128)(2,1)S(1)}, u32[]{:S(2)}, u32[]{:S(2)}) %collective-permute-start.2) | collective-permute-done | bytes 69664 | tf_op jit(solution)/shard_map/ppermute | solution.py:38
  29.6 0.9 pad_maximum_fusion.7
  30.5 1.9 %collective-permute-start.3 = (bf16[544,128]{1,0:T(8,128)(2,1)S(1)}, bf16[544,128]{1,0:T(8,128)(2,1)S(1)}, u32[]{:S(2)}, u32[]{:S(2)}) collective-permute-start(bf16[544,128]{1,0:T(8,128)(2,1)S(1)} %pad_maximum_fusion.7), channel_id=1, source_target_pairs={{0,256},{1,257},{2,258},{3,259},{4,260},{5,261},{6,262},{7,263},{8... | collective-permute-start | bytes 417800 | tf_op jit(solution)/shard_map/ppermute | solution.py:38
  33.1 0.9 pad_maximum_fusion.6
  34.0 14.6 %collective-permute-start.1 = (bf16[800,128]{1,0:T(8,128)(2,1)S(1)}, bf16[800,128]{1,0:T(8,128)(2,1)S(1)}, u32[]{:S(2)}, u32[]{:S(2)}) collective-permute-start(bf16[800,128]{1,0:T(8,128)(2,1)S(1)} %pad_maximum_fusion.6), channel_id=1, source_target_pairs={{0,1},{1,0},{2,3},{3,2},{4,5},{5,4},{6,7},{7,6},{8,9},{9,8},{10,11... | collective-permute-start | bytes 614408 | tf_op jit(solution)/shard_map/ppermute | solution.py:38
  48.6 1.9 %collective-permute-start.4 = (bf16[1088,128]{1,0:T(8,128)(2,1)S(1)}, bf16[1088,128]{1,0:T(8,128)(2,1)S(1)}, u32[]{:S(2)}, u32[]{:S(2)}) collective-permute-start(bf16[1088,128]{1,0:T(8,128)(2,1)S(1)} %pad_maximum_fusion.5), channel_id=1, source_target_pairs={{0,128},{1,129},{2,130},{3,131},{4,132},{5,133},{6,134},{7,135},{8... | collective-permute-start | bytes 835592 | tf_op jit(solution)/shard_map/ppermute | solution.py:38
  50.5 0.7 constant_dynamic-update-slice_fusion.7
  51.2 8.1 %collective-permute-done.1 = bf16[800,128]{1,0:T(8,128)(2,1)S(1)} collective-permute-done((bf16[800,128]{1,0:T(8,128)(2,1)S(1)}, bf16[800,128]{1,0:T(8,128)(2,1)S(1)}, u32[]{:S(2)}, u32[]{:S(2)}) %collective-permute-start.1) | collective-permute-done | bytes 204832 | tf_op jit(solution)/shard_map/ppermute | solution.py:38
  59.9 1.3 hold.1
  61.2 11.1 %collective-permute-done.4 = bf16[1088,128]{1,0:T(8,128)(2,1)S(1)} collective-permute-done((bf16[1088,128]{1,0:T(8,128)(2,1)S(1)}, bf16[1088,128]{1,0:T(8,128)(2,1)S(1)}, u32[]{:S(2)}, u32[]{:S(2)}) %collective-permute-start.4) | collective-permute-done | bytes 278560 | tf_op jit(solution)/shard_map/ppermute | solution.py:38
  72.3 0.8 constant_dynamic-update-slice_fusion.6
  73.0 0.8 constant_dynamic-update-slice_fusion.13
  73.8 1.9 %collective-permute-start.5 = (bf16[2976,128]{1,0:T(8,128)(2,1)S(1)}, bf16[2976,128]{1,0:T(8,128)(2,1)S(1)}, u32[]{:S(2)}, u32[]{:S(2)}) collective-permute-start(bf16[2976,128]{1,0:T(8,128)(2,1)S(1)} %slice_dynamic-update-slice_fusion), channel_id=1, source_target_pairs={{0,16},{1,17},{2,18},{3,19},{4,20},{5,21},{6,22},{7,23},{8,24},{9,... | collective-permute-start | bytes 2285576 | tf_op jit(solution)/shard_map/ppermute | solution.py:38
  75.8 3.8 %collective-permute-start.7 = (bf16[400,128]{1,0:T(8,128)(2,1)S(1)}, bf16[400,128]{1,0:T(8,128)(2,1)S(1)}, u32[]{:S(2)}, u32[]{:S(2)}) collective-permute-start(bf16[400,128]{1,0:T(8,128)(2,1)S(1)} %get-tuple-element.28), channel_id=1, source_target_pairs={{0,3},{1,2},{2,1},{3,0},{4,7},{5,6},{6,5},{7,4},{8,11},{9,10},{10,... | collective-permute-start | bytes 307208 | tf_op jit(solution)/shard_map/ppermute | solution.py:38
  79.7 4.4 %collective-permute-start.6 = (bf16[4352,128]{1,0:T(8,128)(2,1)S(1)}, bf16[4352,128]{1,0:T(8,128)(2,1)S(1)}, u32[]{:S(2)}, u32[]{:S(2)}) collective-permute-start(bf16[4352,128]{1,0:T(8,128)(2,1)S(1)} %get-tuple-element.20), channel_id=1, source_target_pairs={{0,32},{1,33},{2,34},{3,35},{4,36},{5,37},{6,38},{7,39},{8,40},{9,... | collective-permute-start | bytes 3342344 | tf_op jit(solution)/shard_map/ppermute | solution.py:38
  84.2 10.2 %collective-permute-done.7 = bf16[400,128]{1,0:T(8,128)(2,1)S(1)} collective-permute-done((bf16[400,128]{1,0:T(8,128)(2,1)S(1)}, bf16[400,128]{1,0:T(8,128)(2,1)S(1)}, u32[]{:S(2)}, u32[]{:S(2)}) %collective-permute-start.7) | collective-permute-done | bytes 102432 | tf_op jit(solution)/shard_map/ppermute | solution.py:38
  94.4 4.1 %collective-permute-start.8 = (bf16[2400,128]{1,0:T(8,128)(2,1)S(1)}, bf16[2400,128]{1,0:T(8,128)(2,1)S(1)}, u32[]{:S(2)}, u32[]{:S(2)}) collective-permute-start(bf16[2400,128]{1,0:T(8,128)(2,1)S(1)} %constant_dynamic-update-slice_fusion.10), channel_id=1, source_target_pairs={{0,4},{1,5},{2,6},{3,7},{4,0},{5,1},{6,2},{7,3},{8,12},{9,13},{10,... | collective-permute-start | bytes 1843208 | tf_op jit(solution)/shard_map/ppermute | solution.py:38
  98.5 2.4 %collective-permute-start.9 = (bf16[400,128]{1,0:T(8,128)(2,1)S(1)}, bf16[400,128]{1,0:T(8,128)(2,1)S(1)}, u32[]{:S(2)}, u32[]{:S(2)}) collective-permute-start(bf16[400,128]{1,0:T(8,128)(2,1)S(1)} %collective-permute-done.7), channel_id=1, source_target_pairs={{0,4},{1,5},{2,6},{3,7},{4,0},{5,1},{6,2},{7,3},{8,12},{9,13},{10,... | collective-permute-start | bytes 307208 | tf_op jit(solution)/shard_map/ppermute | solution.py:38
  100.9 6.7 %collective-permute-done.9 = bf16[400,128]{1,0:T(8,128)(2,1)S(1)} collective-permute-done((bf16[400,128]{1,0:T(8,128)(2,1)S(1)}, bf16[400,128]{1,0:T(8,128)(2,1)S(1)}, u32[]{:S(2)}, u32[]{:S(2)}) %collective-permute-start.9) | collective-permute-done | bytes 102432 | tf_op jit(solution)/shard_map/ppermute | solution.py:38
  107.8 1.9 %collective-permute-start.11 = (bf16[5552,128]{1,0:T(8,128)(2,1)S(1)}, bf16[5552,128]{1,0:T(8,128)(2,1)S(1)}, u32[]{:S(2)}, u32[]{:S(2)}) collective-permute-start(bf16[5552,128]{1,0:T(8,128)(2,1)S(1)} %pad_maximum_fusion), channel_id=1, source_target_pairs={{0,16},{1,17},{2,18},{3,19},{4,20},{5,21},{6,22},{7,23},{8,24},{9,... | collective-permute-start | bytes 4263944 | tf_op jit(solution)/shard_map/ppermute | solution.py:38
  109.8 2.7 %collective-permute-start.12 = (bf16[2176,128]{1,0:T(8,128)(2,1)S(1)}, bf16[2176,128]{1,0:T(8,128)(2,1)S(1)}, u32[]{:S(2)}, u32[]{:S(2)}) collective-permute-start(bf16[2176,128]{1,0:T(8,128)(2,1)S(1)} %slice.59), channel_id=1, source_target_pairs={{0,96},{1,97},{2,98},{3,99},{4,100},{5,101},{6,102},{7,103},{8,104... | collective-permute-start | bytes 1671176 | tf_op jit(solution)/shard_map/ppermute | solution.py:38
  112.5 2.7 %collective-permute-start.10 = (bf16[2000,128]{1,0:T(8,128)(2,1)S(1)}, bf16[2000,128]{1,0:T(8,128)(2,1)S(1)}, u32[]{:S(2)}, u32[]{:S(2)}) collective-permute-start(bf16[2000,128]{1,0:T(8,128)(2,1)S(1)} %pad_maximum_fusion.2), channel_id=1, source_target_pairs={{0,12},{1,13},{2,14},{3,15},{4,8},{5,9},{6,10},{7,11},{8,4},{9,5},... | collective-permute-start | bytes 1536008 | tf_op jit(solution)/shard_map/ppermute | solution.py:38
  115.2 5.2 %collective-permute-done.12 = bf16[2176,128]{1,0:T(8,128)(2,1)S(1)} collective-permute-done((bf16[2176,128]{1,0:T(8,128)(2,1)S(1)}, bf16[2176,128]{1,0:T(8,128)(2,1)S(1)}, u32[]{:S(2)}, u32[]{:S(2)}) %collective-permute-start.12) | collective-permute-done | bytes 557088 | tf_op jit(solution)/shard_map/ppermute | solution.py:38
  120.5 4.5 %collective-permute-start.13 = (bf16[2176,128]{1,0:T(8,128)(2,1)S(1)}, bf16[2176,128]{1,0:T(8,128)(2,1)S(1)}, u32[]{:S(2)}, u32[]{:S(2)}) collective-permute-start(bf16[2176,128]{1,0:T(8,128)(2,1)S(1)} %collective-permute-done.12), channel_id=1, source_target_pairs={{0,16},{1,17},{2,18},{3,19},{4,20},{5,21},{6,22},{7,23},{8,24},{9,... | collective-permute-start | bytes 1671176 | tf_op jit(solution)/shard_map/ppermute | solution.py:38
  125.2 1.3 collective-permute-done.13
  126.5 6.3 %block_products.1 = bf16[256,1024]{1,0:T(8,128)(2,1)} custom-call(s32[2,8]{1,0:T(2,128)S(1)} %copy-done, bf16[3,400,128]{2,1,0:T(8,128)(2,1)S(1)} %bitcast.17, bf16[3,400,128]{2,1,0:T(8,128)(2,1)S(1)} %bitcast.14, bf16[5,400,128]{2,1,0:T(8,128)(2,1)S(1)} %bitcast.21, bf16[3,400,128]{2,1,0:T(8,128)(2,1)S(1)} %bitcast.18, bf16[1,400,128]{2,1,0:T(8,128)(2,1)S(1)} %bitcast.22, ...), custom_call_target="tpu_custom_call" | custom-call | tf_op jit(solution)/shard_map/block_products/pallas_call | solution.py:317
  (35 shorter events, 1.9 us)
Async XLA Ops:
  3.6 45.0 %copy-start.1 = (bf16[272,128]{1,0:T(8,128)(2,1)S(1)}, bf16[272,128]{1,0:T(8,128)(2,1)}, u32[]{:S(2)}) copy-start(bf16[272,128]{1,0:T(8,128)(2,1)} %get-tuple-element.13) | copy-start | bytes 208900
  3.6 29.5 %collective-permute-start = (bf16[400,128]{1,0:T(8,128)(2,1)}, bf16[400,128]{1,0:T(8,128)(2,1)S(1)}, u32[]{:S(2)}, u32[]{:S(2)}) collective-permute-start(bf16[400,128]{1,0:T(8,128)(2,1)} %get-tuple-element.12), channel_id=1, source_target_pairs={{0,16},{1,17},{2,18},{3,19},{4,20},{5,21},{6,22},{7,23},{8,24},{9,... | collective-permute-start | bytes 307208 | tf_op jit(solution)/shard_map/ppermute | solution.py:38
  19.8 9.8 %collective-permute-start.2 = (bf16[272,128]{1,0:T(8,128)(2,1)}, bf16[272,128]{1,0:T(8,128)(2,1)S(1)}, u32[]{:S(2)}, u32[]{:S(2)}) collective-permute-start(bf16[272,128]{1,0:T(8,128)(2,1)} %get-tuple-element.13), channel_id=1, source_target_pairs={{0,512},{1,513},{2,514},{3,515},{4,516},{5,517},{6,518},{7,519},{8... | collective-permute-start | bytes 208904 | tf_op jit(solution)/shard_map/ppermute | solution.py:38
  30.5 18.0 %collective-permute-start.3 = (bf16[544,128]{1,0:T(8,128)(2,1)S(1)}, bf16[544,128]{1,0:T(8,128)(2,1)S(1)}, u32[]{:S(2)}, u32[]{:S(2)}) collective-permute-start(bf16[544,128]{1,0:T(8,128)(2,1)S(1)} %pad_maximum_fusion.7), channel_id=1, source_target_pairs={{0,256},{1,257},{2,258},{3,259},{4,260},{5,261},{6,262},{7,263},{8... | collective-permute-start | bytes 417800 | tf_op jit(solution)/shard_map/ppermute | solution.py:38
  34.0 25.4 %collective-permute-start.1 = (bf16[800,128]{1,0:T(8,128)(2,1)S(1)}, bf16[800,128]{1,0:T(8,128)(2,1)S(1)}, u32[]{:S(2)}, u32[]{:S(2)}) collective-permute-start(bf16[800,128]{1,0:T(8,128)(2,1)S(1)} %pad_maximum_fusion.6), channel_id=1, source_target_pairs={{0,1},{1,0},{2,3},{3,2},{4,5},{5,4},{6,7},{7,6},{8,9},{9,8},{10,11... | collective-permute-start | bytes 614408 | tf_op jit(solution)/shard_map/ppermute | solution.py:38
  48.6 23.7 %collective-permute-start.4 = (bf16[1088,128]{1,0:T(8,128)(2,1)S(1)}, bf16[1088,128]{1,0:T(8,128)(2,1)S(1)}, u32[]{:S(2)}, u32[]{:S(2)}) collective-permute-start(bf16[1088,128]{1,0:T(8,128)(2,1)S(1)} %pad_maximum_fusion.5), channel_id=1, source_target_pairs={{0,128},{1,129},{2,130},{3,131},{4,132},{5,133},{6,134},{7,135},{8... | collective-permute-start | bytes 835592 | tf_op jit(solution)/shard_map/ppermute | solution.py:38
  73.0 6.6 %copy-start.4 = (bf16[4352,128]{1,0:T(8,128)(2,1)S(1)}, bf16[4352,128]{1,0:T(8,128)(2,1)}, u32[]{:S(2)}) copy-start(bf16[4352,128]{1,0:T(8,128)(2,1)} %get-tuple-element.26) | copy-start | bytes 3342340
  73.8 5.8 %collective-permute-start.5 = (bf16[2976,128]{1,0:T(8,128)(2,1)S(1)}, bf16[2976,128]{1,0:T(8,128)(2,1)S(1)}, u32[]{:S(2)}, u32[]{:S(2)}) collective-permute-start(bf16[2976,128]{1,0:T(8,128)(2,1)S(1)} %slice_dynamic-update-slice_fusion), channel_id=1, source_target_pairs={{0,16},{1,17},{2,18},{3,19},{4,20},{5,21},{6,22},{7,23},{8,24},{9,... | collective-permute-start | bytes 2285576 | tf_op jit(solution)/shard_map/ppermute | solution.py:38
  75.8 18.6 %collective-permute-start.7 = (bf16[400,128]{1,0:T(8,128)(2,1)S(1)}, bf16[400,128]{1,0:T(8,128)(2,1)S(1)}, u32[]{:S(2)}, u32[]{:S(2)}) collective-permute-start(bf16[400,128]{1,0:T(8,128)(2,1)S(1)} %get-tuple-element.28), channel_id=1, source_target_pairs={{0,3},{1,2},{2,1},{3,0},{4,7},{5,6},{6,5},{7,4},{8,11},{9,10},{10,... | collective-permute-start | bytes 307208 | tf_op jit(solution)/shard_map/ppermute | solution.py:38
  79.7 27.9 %collective-permute-start.6 = (bf16[4352,128]{1,0:T(8,128)(2,1)S(1)}, bf16[4352,128]{1,0:T(8,128)(2,1)S(1)}, u32[]{:S(2)}, u32[]{:S(2)}) collective-permute-start(bf16[4352,128]{1,0:T(8,128)(2,1)S(1)} %get-tuple-element.20), channel_id=1, source_target_pairs={{0,32},{1,33},{2,34},{3,35},{4,36},{5,37},{6,38},{7,39},{8,40},{9,... | collective-permute-start | bytes 3342344 | tf_op jit(solution)/shard_map/ppermute | solution.py:38
  94.4 13.2 %collective-permute-start.8 = (bf16[2400,128]{1,0:T(8,128)(2,1)S(1)}, bf16[2400,128]{1,0:T(8,128)(2,1)S(1)}, u32[]{:S(2)}, u32[]{:S(2)}) collective-permute-start(bf16[2400,128]{1,0:T(8,128)(2,1)S(1)} %constant_dynamic-update-slice_fusion.10), channel_id=1, source_target_pairs={{0,4},{1,5},{2,6},{3,7},{4,0},{5,1},{6,2},{7,3},{8,12},{9,13},{10,... | collective-permute-start | bytes 1843208 | tf_op jit(solution)/shard_map/ppermute | solution.py:38
  98.5 9.1 %collective-permute-start.9 = (bf16[400,128]{1,0:T(8,128)(2,1)S(1)}, bf16[400,128]{1,0:T(8,128)(2,1)S(1)}, u32[]{:S(2)}, u32[]{:S(2)}) collective-permute-start(bf16[400,128]{1,0:T(8,128)(2,1)S(1)} %collective-permute-done.7), channel_id=1, source_target_pairs={{0,4},{1,5},{2,6},{3,7},{4,0},{5,1},{6,2},{7,3},{8,12},{9,13},{10,... | collective-permute-start | bytes 307208 | tf_op jit(solution)/shard_map/ppermute | solution.py:38
  107.8 17.3 %collective-permute-start.11 = (bf16[5552,128]{1,0:T(8,128)(2,1)S(1)}, bf16[5552,128]{1,0:T(8,128)(2,1)S(1)}, u32[]{:S(2)}, u32[]{:S(2)}) collective-permute-start(bf16[5552,128]{1,0:T(8,128)(2,1)S(1)} %pad_maximum_fusion), channel_id=1, source_target_pairs={{0,16},{1,17},{2,18},{3,19},{4,20},{5,21},{6,22},{7,23},{8,24},{9,... | collective-permute-start | bytes 4263944 | tf_op jit(solution)/shard_map/ppermute | solution.py:38
  109.7 15.2 %copy-start.2 = (bf16[400,128]{1,0:T(8,128)(2,1)S(1)}, bf16[400,128]{1,0:T(8,128)(2,1)}, u32[]{:S(2)}) copy-start(bf16[400,128]{1,0:T(8,128)(2,1)} %get-tuple-element.12) | copy-start | bytes 307204
  109.8 15.2 %copy-start.3 = (bf16[16,128]{1,0:T(8,128)(2,1)S(1)}, bf16[16,128]{1,0:T(8,128)(2,1)}, u32[]{:S(2)}) copy-start(bf16[16,128]{1,0:T(8,128)(2,1)} %hold.1) | copy-start | bytes 12292
  109.8 10.7 %collective-permute-start.12 = (bf16[2176,128]{1,0:T(8,128)(2,1)S(1)}, bf16[2176,128]{1,0:T(8,128)(2,1)S(1)}, u32[]{:S(2)}, u32[]{:S(2)}) collective-permute-start(bf16[2176,128]{1,0:T(8,128)(2,1)S(1)} %slice.59), channel_id=1, source_target_pairs={{0,96},{1,97},{2,98},{3,99},{4,100},{5,101},{6,102},{7,103},{8,104... | collective-permute-start | bytes 1671176 | tf_op jit(solution)/shard_map/ppermute | solution.py:38
  112.5 12.6 %collective-permute-start.10 = (bf16[2000,128]{1,0:T(8,128)(2,1)S(1)}, bf16[2000,128]{1,0:T(8,128)(2,1)S(1)}, u32[]{:S(2)}, u32[]{:S(2)}) collective-permute-start(bf16[2000,128]{1,0:T(8,128)(2,1)S(1)} %pad_maximum_fusion.2), channel_id=1, source_target_pairs={{0,12},{1,13},{2,14},{3,15},{4,8},{5,9},{6,10},{7,11},{8,4},{9,5},... | collective-permute-start | bytes 1536008 | tf_op jit(solution)/shard_map/ppermute | solution.py:38
  120.5 6.0 %collective-permute-start.13 = (bf16[2176,128]{1,0:T(8,128)(2,1)S(1)}, bf16[2176,128]{1,0:T(8,128)(2,1)S(1)}, u32[]{:S(2)}, u32[]{:S(2)}) collective-permute-start(bf16[2176,128]{1,0:T(8,128)(2,1)S(1)} %collective-permute-done.12), channel_id=1, source_target_pairs={{0,16},{1,17},{2,18},{3,19},{4,20},{5,21},{6,22},{7,23},{8,24},{9,... | collective-permute-start | bytes 1671176 | tf_op jit(solution)/shard_map/ppermute | solution.py:38
  125.1 1.4 %copy-start = (s32[2,8]{1,0:T(2,128)S(1)}, s32[2,8]{1,0:T(2,128)}, u32[]{:S(2)}) copy-start(s32[2,8]{1,0:T(2,128)} %refs_0_.1) | copy-start | bytes 196

commit v3 on v2

--- a/solution.py
+++ b/solution.py
@@ -142,14 +142,14 @@
     others, z_two = lax.optimization_barrier((others, z_two))
     y_one = y_swap(cat([mine, others]), 1, 3)
     z_near = y_swap(z_two, 1, 3)
-    x_one, y_one, z_near = lax.optimization_barrier((x_one, y_one, z_near))
+    y_one, z_near = lax.optimization_barrier((y_one, z_near))
     x_two = x_swap(x_one[:high], 3, 1)
+    x_other = core_swap(x_one)
     y_two = y_swap(cat([y_one[: 3 * rows], z_two, z_near]), 3, 1)
-    swapped = core_swap(cat([x_one, y_one[3 * rows :]]))
-    x_last = core_swap(x_two)
+    swapped = core_swap(cat([x_two, y_one[3 * rows :]]))
     return (
-        [mine, y_one[: 3 * rows], y_two, swapped[2 * high :], z_two, z_near],
-        [right, near_right, x_one, swapped[: 2 * high], x_two, x_last],
+        [mine, y_one[: 3 * rows], y_two, swapped[high:], z_two, z_near],
+        [right, near_right, x_one, x_other, x_two, swapped[:high]],
     )
 
 

time: 134 us -> 135 us (level)
  waiting for transfers between devices: 48.1 us -> 40.4 us
  starting transfers between devices: 64.9 us -> 72.3 us
    ppermute x14, waiting for transfers between devices: 48.1 us -> 40.4 us  [swap(): return lax.ppermute(value, ('row', 'col'), pairs(partner))]
    ppermute x14, starting transfers between devices: 64.9 us -> 72.3 us  [swap(): return lax.ppermute(value, ('row', 'col'), pairs(partner))]
  transfers between devices with their start and end apart: 14 -> 14, of which waited for: 7 -> 6; matrix products, arithmetic and copies ran while one was open for 5% -> 5% of each run, Pallas kernels for 1% -> 1%
where the time goes in v3:
time: 135 us; the launch traced here: 133 us
  starting transfers between devices  72.3 us (54%)
  waiting for transfers between devices  40.4 us (30%)
  Pallas kernels  9.95 us (7%)
  local copies, waits for them, and re-layouts  7.62 us (6%)
  other arithmetic  2 us (1%)
    ppermute x14, starting transfers between devices, swap(): return lax.ppermute(value, ('row', 'col'), pairs(partner))  72.3 us
    ppermute x14, waiting for transfers between devices, swap(): return lax.ppermute(value, ('row', 'col'), pairs(partner))  40.4 us
    unnamed x18, local copies, waits for them, and re-layouts  6.65 us
    pallas_call x1, Pallas kernels, multiply_parts(): pl.pallas_call(kernel, out_shape=jax.ShapeDtypeStruct((band * BLK, slab *...  6.44 us
  transfers between devices with their start and end apart: 14, of which 6 were waited for; matrix products, arithmetic and copies ran while one was open for 5% of the time, Pallas kernels for 1%

profile of v3, /device:TPU:1, one launch (start us, length us, event | category | flops | bytes accessed | tf_op | source)
XLA Modules:
  0.0 132.6 jit_solution(2635954404025128011)
XLA Ops:
  0.0 1.3 %copy.6.left_index = s32[3,2]{1,0:T(4,128)} copy(s32[3,2]{0,1:T(2,128)} %param.6) | data formatting | bytes 48 | tf_op args[1]
  1.3 2.2 %pack.1 = (bf16[400,128]{1,0:T(8,128)(2,1)}, bf16[272,128]{1,0:T(8,128)(2,1)}) custom-call(s32[3,2]{1,0:T(4,128)} %copy.6.left_index, s32[2,2]{1,0:T(2,128)} %right_index.1, bf16[3,128,128]{2,1,0:T(8,128)(2,1)} %left_blocks.1, bf16[2,128,128]{2,1,0:T(8,128)(2,1)} %right_blocks.1), custom_call_target="tpu_custom_call" | custom-call | tf_op jit(solution)/shard_map/pack/pallas_call | solution.py:112
  3.6 9.8 %collective-permute-start.2 = (bf16[272,128]{1,0:T(8,128)(2,1)}, bf16[272,128]{1,0:T(8,128)(2,1)S(1)}, u32[]{:S(2)}, u32[]{:S(2)}) collective-permute-start(bf16[272,128]{1,0:T(8,128)(2,1)} %get-tuple-element.12), channel_id=1, source_target_pairs={{0,512},{1,513},{2,514},{3,515},{4,516},{5,517},{6,518},{7,519},{8... | collective-permute-start | bytes 208904 | tf_op jit(solution)/shard_map/ppermute | solution.py:38
  13.4 8.3 %collective-permute-start = (bf16[400,128]{1,0:T(8,128)(2,1)}, bf16[400,128]{1,0:T(8,128)(2,1)S(1)}, u32[]{:S(2)}, u32[]{:S(2)}) collective-permute-start(bf16[400,128]{1,0:T(8,128)(2,1)} %get-tuple-element.11), channel_id=1, source_target_pairs={{0,16},{1,17},{2,18},{3,19},{4,20},{5,21},{6,22},{7,23},{8,24},{9,... | collective-permute-start | bytes 307208 | tf_op jit(solution)/shard_map/ppermute | solution.py:38
  21.7 1.5 %constant_dynamic-update-slice_fusion.14 = (bf16[4352,128]{1,0:T(8,128)(2,1)}, bf16[2976,128]{1,0:T(8,128)(2,1)S(1)}) fusion(bf16[272,128]{1,0:T(8,128)(2,1)} %get-tuple-element.12), kind=kLoop, calls=%fused_computation.23 | loop fusion | bytes 208896
  23.2 0.9 constant_dynamic-update-slice_fusion.9
  24.2 0.9 pad_maximum_fusion.7
  25.1 1.9 %collective-permute-start.3 = (bf16[544,128]{1,0:T(8,128)(2,1)S(1)}, bf16[544,128]{1,0:T(8,128)(2,1)S(1)}, u32[]{:S(2)}, u32[]{:S(2)}) collective-permute-start(bf16[544,128]{1,0:T(8,128)(2,1)S(1)} %pad_maximum_fusion.7), channel_id=1, source_target_pairs={{0,256},{1,257},{2,258},{3,259},{4,260},{5,261},{6,262},{7,263},{8... | collective-permute-start | bytes 417800 | tf_op jit(solution)/shard_map/ppermute | solution.py:38
  27.0 0.6 constant_dynamic-update-slice_fusion.13
  27.6 0.9 pad_maximum_fusion.6
  28.5 17.2 %collective-permute-start.1 = (bf16[800,128]{1,0:T(8,128)(2,1)S(1)}, bf16[800,128]{1,0:T(8,128)(2,1)S(1)}, u32[]{:S(2)}, u32[]{:S(2)}) collective-permute-start(bf16[800,128]{1,0:T(8,128)(2,1)S(1)} %pad_maximum_fusion.6), channel_id=1, source_target_pairs={{0,1},{1,0},{2,3},{3,2},{4,5},{5,4},{6,7},{7,6},{8,9},{9,8},{10,11... | collective-permute-start | bytes 614408 | tf_op jit(solution)/shard_map/ppermute | solution.py:38
  45.8 1.9 %collective-permute-start.4 = (bf16[1088,128]{1,0:T(8,128)(2,1)S(1)}, bf16[1088,128]{1,0:T(8,128)(2,1)S(1)}, u32[]{:S(2)}, u32[]{:S(2)}) collective-permute-start(bf16[1088,128]{1,0:T(8,128)(2,1)S(1)} %pad_maximum_fusion.5), channel_id=1, source_target_pairs={{0,128},{1,129},{2,130},{3,131},{4,132},{5,133},{6,134},{7,135},{8... | collective-permute-start | bytes 835592 | tf_op jit(solution)/shard_map/ppermute | solution.py:38
  47.7 0.7 constant_dynamic-update-slice_fusion.12
  48.4 7.9 %collective-permute-done.1 = bf16[800,128]{1,0:T(8,128)(2,1)S(1)} collective-permute-done((bf16[800,128]{1,0:T(8,128)(2,1)S(1)}, bf16[800,128]{1,0:T(8,128)(2,1)S(1)}, u32[]{:S(2)}, u32[]{:S(2)}) %collective-permute-start.1) | collective-permute-done | bytes 204832 | tf_op jit(solution)/shard_map/ppermute | solution.py:38
  56.9 1.3 hold.1
  58.2 11.3 %collective-permute-done.4 = bf16[1088,128]{1,0:T(8,128)(2,1)S(1)} collective-permute-done((bf16[1088,128]{1,0:T(8,128)(2,1)S(1)}, bf16[1088,128]{1,0:T(8,128)(2,1)S(1)}, u32[]{:S(2)}, u32[]{:S(2)}) %collective-permute-start.4) | collective-permute-done | bytes 278560 | tf_op jit(solution)/shard_map/ppermute | solution.py:38
  69.5 0.8 constant_dynamic-update-slice_fusion.11
  70.3 0.8 constant_dynamic-update-slice_fusion.8
  71.1 1.9 %collective-permute-start.5 = (bf16[2976,128]{1,0:T(8,128)(2,1)S(1)}, bf16[2976,128]{1,0:T(8,128)(2,1)S(1)}, u32[]{:S(2)}, u32[]{:S(2)}) collective-permute-start(bf16[2976,128]{1,0:T(8,128)(2,1)S(1)} %slice_dynamic-update-slice_fusion), channel_id=1, source_target_pairs={{0,16},{1,17},{2,18},{3,19},{4,20},{5,21},{6,22},{7,23},{8,24},{9,... | collective-permute-start | bytes 2285576 | tf_op jit(solution)/shard_map/ppermute | solution.py:38
  73.0 6.5 %collective-permute-start.6 = (bf16[400,128]{1,0:T(8,128)(2,1)S(1)}, bf16[400,128]{1,0:T(8,128)(2,1)S(1)}, u32[]{:S(2)}, u32[]{:S(2)}) collective-permute-start(bf16[400,128]{1,0:T(8,128)(2,1)S(1)} %get-tuple-element.26), channel_id=1, source_target_pairs={{0,3},{1,2},{2,1},{3,0},{4,7},{5,6},{6,5},{7,4},{8,11},{9,10},{10,... | collective-permute-start | bytes 307208 | tf_op jit(solution)/shard_map/ppermute | solution.py:38
  79.7 4.4 %collective-permute-start.10 = (bf16[4352,128]{1,0:T(8,128)(2,1)S(1)}, bf16[4352,128]{1,0:T(8,128)(2,1)S(1)}, u32[]{:S(2)}, u32[]{:S(2)}) collective-permute-start(bf16[4352,128]{1,0:T(8,128)(2,1)S(1)} %get-tuple-element.18), channel_id=1, source_target_pairs={{0,32},{1,33},{2,34},{3,35},{4,36},{5,37},{6,38},{7,39},{8,40},{9,... | collective-permute-start | bytes 3342344 | tf_op jit(solution)/shard_map/ppermute | solution.py:38
  84.1 8.6 %collective-permute-done.6 = bf16[400,128]{1,0:T(8,128)(2,1)S(1)} collective-permute-done((bf16[400,128]{1,0:T(8,128)(2,1)S(1)}, bf16[400,128]{1,0:T(8,128)(2,1)S(1)}, u32[]{:S(2)}, u32[]{:S(2)}) %collective-permute-start.6) | collective-permute-done | bytes 102432 | tf_op jit(solution)/shard_map/ppermute | solution.py:38
  92.8 4.2 %collective-permute-start.7 = (bf16[2400,128]{1,0:T(8,128)(2,1)S(1)}, bf16[2400,128]{1,0:T(8,128)(2,1)S(1)}, u32[]{:S(2)}, u32[]{:S(2)}) collective-permute-start(bf16[2400,128]{1,0:T(8,128)(2,1)S(1)} %constant_dynamic-update-slice_fusion.5), channel_id=1, source_target_pairs={{0,4},{1,5},{2,6},{3,7},{4,0},{5,1},{6,2},{7,3},{8,12},{9,13},{10,... | collective-permute-start | bytes 1843208 | tf_op jit(solution)/shard_map/ppermute | solution.py:38
  96.9 2.3 %collective-permute-start.8 = (bf16[400,128]{1,0:T(8,128)(2,1)S(1)}, bf16[400,128]{1,0:T(8,128)(2,1)S(1)}, u32[]{:S(2)}, u32[]{:S(2)}) collective-permute-start(bf16[400,128]{1,0:T(8,128)(2,1)S(1)} %collective-permute-done.6), channel_id=1, source_target_pairs={{0,4},{1,5},{2,6},{3,7},{4,0},{5,1},{6,2},{7,3},{8,12},{9,13},{10,... | collective-permute-start | bytes 307208 | tf_op jit(solution)/shard_map/ppermute | solution.py:38
  99.3 2.7 %collective-permute-start.11 = (bf16[2176,128]{1,0:T(8,128)(2,1)S(1)}, bf16[2176,128]{1,0:T(8,128)(2,1)S(1)}, u32[]{:S(2)}, u32[]{:S(2)}) collective-permute-start(bf16[2176,128]{1,0:T(8,128)(2,1)S(1)} %slice.68), channel_id=1, source_target_pairs={{0,96},{1,97},{2,98},{3,99},{4,100},{5,101},{6,102},{7,103},{8,104... | collective-permute-start | bytes 1671176 | tf_op jit(solution)/shard_map/ppermute | solution.py:38
  102.1 3.9 %collective-permute-done.8 = bf16[400,128]{1,0:T(8,128)(2,1)S(1)} collective-permute-done((bf16[400,128]{1,0:T(8,128)(2,1)S(1)}, bf16[400,128]{1,0:T(8,128)(2,1)S(1)}, u32[]{:S(2)}, u32[]{:S(2)}) %collective-permute-start.8) | collective-permute-done | bytes 102432 | tf_op jit(solution)/shard_map/ppermute | solution.py:38
  106.0 1.9 %collective-permute-start.13 = (bf16[4352,128]{1,0:T(8,128)(2,1)S(1)}, bf16[4352,128]{1,0:T(8,128)(2,1)S(1)}, u32[]{:S(2)}, u32[]{:S(2)}) collective-permute-start(bf16[4352,128]{1,0:T(8,128)(2,1)S(1)} %collective-permute-done.10), channel_id=1, source_target_pairs={{0,16},{1,17},{2,18},{3,19},{4,20},{5,21},{6,22},{7,23},{8,24},{9,... | collective-permute-start | bytes 3342344 | tf_op jit(solution)/shard_map/ppermute | solution.py:38
  107.9 2.0 %collective-permute-done.11 = bf16[2176,128]{1,0:T(8,128)(2,1)S(1)} collective-permute-done((bf16[2176,128]{1,0:T(8,128)(2,1)S(1)}, bf16[2176,128]{1,0:T(8,128)(2,1)S(1)}, u32[]{:S(2)}, u32[]{:S(2)}) %collective-permute-start.11) | collective-permute-done | bytes 557088 | tf_op jit(solution)/shard_map/ppermute | solution.py:38
  110.0 6.0 %collective-permute-start.12 = (bf16[3376,128]{1,0:T(8,128)(2,1)S(1)}, bf16[3376,128]{1,0:T(8,128)(2,1)S(1)}, u32[]{:S(2)}, u32[]{:S(2)}) collective-permute-start(bf16[3376,128]{1,0:T(8,128)(2,1)S(1)} %pad_maximum_fusion), channel_id=1, source_target_pairs={{0,16},{1,17},{2,18},{3,19},{4,20},{5,21},{6,22},{7,23},{8,24},{9,... | collective-permute-start | bytes 2592776 | tf_op jit(solution)/shard_map/ppermute | solution.py:38
  116.1 3.2 %collective-permute-start.9 = (bf16[2000,128]{1,0:T(8,128)(2,1)S(1)}, bf16[2000,128]{1,0:T(8,128)(2,1)S(1)}, u32[]{:S(2)}, u32[]{:S(2)}) collective-permute-start(bf16[2000,128]{1,0:T(8,128)(2,1)S(1)} %pad_maximum_fusion.2), channel_id=1, source_target_pairs={{0,12},{1,13},{2,14},{3,15},{4,8},{5,9},{6,10},{7,11},{8,4},{9,5},... | collective-permute-start | bytes 1536008 | tf_op jit(solution)/shard_map/ppermute | solution.py:38
  119.5 6.7 %collective-permute-done.9 = bf16[2000,128]{1,0:T(8,128)(2,1)S(1)} collective-permute-done((bf16[2000,128]{1,0:T(8,128)(2,1)S(1)}, bf16[2000,128]{1,0:T(8,128)(2,1)S(1)}, u32[]{:S(2)}, u32[]{:S(2)}) %collective-permute-start.9) | collective-permute-done | bytes 512032 | tf_op jit(solution)/shard_map/ppermute | solution.py:38
  126.2 6.4 %block_products.1 = bf16[256,1024]{1,0:T(8,128)(2,1)} custom-call(s32[2,8]{1,0:T(2,128)S(1)} %copy-done, bf16[3,400,128]{2,1,0:T(8,128)(2,1)S(1)} %bitcast.18, bf16[3,400,128]{2,1,0:T(8,128)(2,1)S(1)} %bitcast.12, bf16[5,400,128]{2,1,0:T(8,128)(2,1)S(1)} %bitcast.21, bf16[3,400,128]{2,1,0:T(8,128)(2,1)S(1)} %bitcast.19, bf16[1,400,128]{2,1,0:T(8,128)(2,1)S(1)} %bitcast.22, ...), custom_call_target="tpu_custom_call" | custom-call | tf_op jit(solution)/shard_map/block_products/pallas_call | solution.py:317
  (35 shorter events, 1.2 us)
Async XLA Ops:
  3.6 42.2 %copy-start.1 = (bf16[272,128]{1,0:T(8,128)(2,1)S(1)}, bf16[272,128]{1,0:T(8,128)(2,1)}, u32[]{:S(2)}) copy-start(bf16[272,128]{1,0:T(8,128)(2,1)} %get-tuple-element.12) | copy-start | bytes 208900
  3.6 20.6 %collective-permute-start.2 = (bf16[272,128]{1,0:T(8,128)(2,1)}, bf16[272,128]{1,0:T(8,128)(2,1)S(1)}, u32[]{:S(2)}, u32[]{:S(2)}) collective-permute-start(bf16[272,128]{1,0:T(8,128)(2,1)} %get-tuple-element.12), channel_id=1, source_target_pairs={{0,512},{1,513},{2,514},{3,515},{4,516},{5,517},{6,518},{7,519},{8... | collective-permute-start | bytes 208904 | tf_op jit(solution)/shard_map/ppermute | solution.py:38
  13.4 14.2 %collective-permute-start = (bf16[400,128]{1,0:T(8,128)(2,1)}, bf16[400,128]{1,0:T(8,128)(2,1)S(1)}, u32[]{:S(2)}, u32[]{:S(2)}) collective-permute-start(bf16[400,128]{1,0:T(8,128)(2,1)} %get-tuple-element.11), channel_id=1, source_target_pairs={{0,16},{1,17},{2,18},{3,19},{4,20},{5,21},{6,22},{7,23},{8,24},{9,... | collective-permute-start | bytes 307208 | tf_op jit(solution)/shard_map/ppermute | solution.py:38
  25.1 20.7 %collective-permute-start.3 = (bf16[544,128]{1,0:T(8,128)(2,1)S(1)}, bf16[544,128]{1,0:T(8,128)(2,1)S(1)}, u32[]{:S(2)}, u32[]{:S(2)}) collective-permute-start(bf16[544,128]{1,0:T(8,128)(2,1)S(1)} %pad_maximum_fusion.7), channel_id=1, source_target_pairs={{0,256},{1,257},{2,258},{3,259},{4,260},{5,261},{6,262},{7,263},{8... | collective-permute-start | bytes 417800 | tf_op jit(solution)/shard_map/ppermute | solution.py:38
  28.5 27.8 %collective-permute-start.1 = (bf16[800,128]{1,0:T(8,128)(2,1)S(1)}, bf16[800,128]{1,0:T(8,128)(2,1)S(1)}, u32[]{:S(2)}, u32[]{:S(2)}) collective-permute-start(bf16[800,128]{1,0:T(8,128)(2,1)S(1)} %pad_maximum_fusion.6), channel_id=1, source_target_pairs={{0,1},{1,0},{2,3},{3,2},{4,5},{5,4},{6,7},{7,6},{8,9},{9,8},{10,11... | collective-permute-start | bytes 614408 | tf_op jit(solution)/shard_map/ppermute | solution.py:38
  45.8 23.7 %collective-permute-start.4 = (bf16[1088,128]{1,0:T(8,128)(2,1)S(1)}, bf16[1088,128]{1,0:T(8,128)(2,1)S(1)}, u32[]{:S(2)}, u32[]{:S(2)}) collective-permute-start(bf16[1088,128]{1,0:T(8,128)(2,1)S(1)} %pad_maximum_fusion.5), channel_id=1, source_target_pairs={{0,128},{1,129},{2,130},{3,131},{4,132},{5,133},{6,134},{7,135},{8... | collective-permute-start | bytes 835592 | tf_op jit(solution)/shard_map/ppermute | solution.py:38
  70.3 9.3 %copy-start.4 = (bf16[4352,128]{1,0:T(8,128)(2,1)S(1)}, bf16[4352,128]{1,0:T(8,128)(2,1)}, u32[]{:S(2)}) copy-start(bf16[4352,128]{1,0:T(8,128)(2,1)} %get-tuple-element.24) | copy-start | bytes 3342340
  71.1 8.4 %collective-permute-start.5 = (bf16[2976,128]{1,0:T(8,128)(2,1)S(1)}, bf16[2976,128]{1,0:T(8,128)(2,1)S(1)}, u32[]{:S(2)}, u32[]{:S(2)}) collective-permute-start(bf16[2976,128]{1,0:T(8,128)(2,1)S(1)} %slice_dynamic-update-slice_fusion), channel_id=1, source_target_pairs={{0,16},{1,17},{2,18},{3,19},{4,20},{5,21},{6,22},{7,23},{8,24},{9,... | collective-permute-start | bytes 2285576 | tf_op jit(solution)/shard_map/ppermute | solution.py:38
  73.0 19.7 %collective-permute-start.6 = (bf16[400,128]{1,0:T(8,128)(2,1)S(1)}, bf16[400,128]{1,0:T(8,128)(2,1)S(1)}, u32[]{:S(2)}, u32[]{:S(2)}) collective-permute-start(bf16[400,128]{1,0:T(8,128)(2,1)S(1)} %get-tuple-element.26), channel_id=1, source_target_pairs={{0,3},{1,2},{2,1},{3,0},{4,7},{5,6},{6,5},{7,4},{8,11},{9,10},{10,... | collective-permute-start | bytes 307208 | tf_op jit(solution)/shard_map/ppermute | solution.py:38
  79.7 19.6 %collective-permute-start.10 = (bf16[4352,128]{1,0:T(8,128)(2,1)S(1)}, bf16[4352,128]{1,0:T(8,128)(2,1)S(1)}, u32[]{:S(2)}, u32[]{:S(2)}) collective-permute-start(bf16[4352,128]{1,0:T(8,128)(2,1)S(1)} %get-tuple-element.18), channel_id=1, source_target_pairs={{0,32},{1,33},{2,34},{3,35},{4,36},{5,37},{6,38},{7,39},{8,40},{9,... | collective-permute-start | bytes 3342344 | tf_op jit(solution)/shard_map/ppermute | solution.py:38
  92.8 13.2 %collective-permute-start.7 = (bf16[2400,128]{1,0:T(8,128)(2,1)S(1)}, bf16[2400,128]{1,0:T(8,128)(2,1)S(1)}, u32[]{:S(2)}, u32[]{:S(2)}) collective-permute-start(bf16[2400,128]{1,0:T(8,128)(2,1)S(1)} %constant_dynamic-update-slice_fusion.5), channel_id=1, source_target_pairs={{0,4},{1,5},{2,6},{3,7},{4,0},{5,1},{6,2},{7,3},{8,12},{9,13},{10,... | collective-permute-start | bytes 1843208 | tf_op jit(solution)/shard_map/ppermute | solution.py:38
  96.9 9.0 %collective-permute-start.8 = (bf16[400,128]{1,0:T(8,128)(2,1)S(1)}, bf16[400,128]{1,0:T(8,128)(2,1)S(1)}, u32[]{:S(2)}, u32[]{:S(2)}) collective-permute-start(bf16[400,128]{1,0:T(8,128)(2,1)S(1)} %collective-permute-done.6), channel_id=1, source_target_pairs={{0,4},{1,5},{2,6},{3,7},{4,0},{5,1},{6,2},{7,3},{8,12},{9,13},{10,... | collective-permute-start | bytes 307208 | tf_op jit(solution)/shard_map/ppermute | solution.py:38
  99.3 10.6 %collective-permute-start.11 = (bf16[2176,128]{1,0:T(8,128)(2,1)S(1)}, bf16[2176,128]{1,0:T(8,128)(2,1)S(1)}, u32[]{:S(2)}, u32[]{:S(2)}) collective-permute-start(bf16[2176,128]{1,0:T(8,128)(2,1)S(1)} %slice.68), channel_id=1, source_target_pairs={{0,96},{1,97},{2,98},{3,99},{4,100},{5,101},{6,102},{7,103},{8,104... | collective-permute-start | bytes 1671176 | tf_op jit(solution)/shard_map/ppermute | solution.py:38
  106.0 20.1 %collective-permute-start.13 = (bf16[4352,128]{1,0:T(8,128)(2,1)S(1)}, bf16[4352,128]{1,0:T(8,128)(2,1)S(1)}, u32[]{:S(2)}, u32[]{:S(2)}) collective-permute-start(bf16[4352,128]{1,0:T(8,128)(2,1)S(1)} %collective-permute-done.10), channel_id=1, source_target_pairs={{0,16},{1,17},{2,18},{3,19},{4,20},{5,21},{6,22},{7,23},{8,24},{9,... | collective-permute-start | bytes 3342344 | tf_op jit(solution)/shard_map/ppermute | solution.py:38
  110.0 9.4 %copy-start.2 = (bf16[400,128]{1,0:T(8,128)(2,1)S(1)}, bf16[400,128]{1,0:T(8,128)(2,1)}, u32[]{:S(2)}) copy-start(bf16[400,128]{1,0:T(8,128)(2,1)} %get-tuple-element.11) | copy-start | bytes 307204
  110.0 9.4 %copy-start.3 = (bf16[16,128]{1,0:T(8,128)(2,1)S(1)}, bf16[16,128]{1,0:T(8,128)(2,1)}, u32[]{:S(2)}) copy-start(bf16[16,128]{1,0:T(8,128)(2,1)} %hold.1) | copy-start | bytes 12292
  110.0 9.4 %collective-permute-start.12 = (bf16[3376,128]{1,0:T(8,128)(2,1)S(1)}, bf16[3376,128]{1,0:T(8,128)(2,1)S(1)}, u32[]{:S(2)}, u32[]{:S(2)}) collective-permute-start(bf16[3376,128]{1,0:T(8,128)(2,1)S(1)} %pad_maximum_fusion), channel_id=1, source_target_pairs={{0,16},{1,17},{2,18},{3,19},{4,20},{5,21},{6,22},{7,23},{8,24},{9,... | collective-permute-start | bytes 2592776 | tf_op jit(solution)/shard_map/ppermute | solution.py:38
  116.1 10.1 %collective-permute-start.9 = (bf16[2000,128]{1,0:T(8,128)(2,1)S(1)}, bf16[2000,128]{1,0:T(8,128)(2,1)S(1)}, u32[]{:S(2)}, u32[]{:S(2)}) collective-permute-start(bf16[2000,128]{1,0:T(8,128)(2,1)S(1)} %pad_maximum_fusion.2), channel_id=1, source_target_pairs={{0,12},{1,13},{2,14},{3,15},{4,8},{5,9},{6,10},{7,11},{8,4},{9,5},... | collective-permute-start | bytes 1536008 | tf_op jit(solution)/shard_map/ppermute | solution.py:38
  119.3 6.8 %copy-start = (s32[2,8]{1,0:T(2,128)S(1)}, s32[2,8]{1,0:T(2,128)}, u32[]{:S(2)}) copy-start(s32[2,8]{1,0:T(2,128)} %refs_0_.1) | copy-start | bytes 196

commit v4 on v3

--- a/solution.py
+++ b/solution.py
@@ -93,9 +93,9 @@
         out[pl.ds(out.shape[0] - META, META), :] = meta.astype(jnp.float32).astype(jnp.bfloat16)
 
     row, col = lax.axis_index("row"), lax.axis_index("col")
-    columns = [left_index[s, 1] for s in range(A_SLOTS)]
+    columns = [left_index[1, s] for s in range(A_SLOTS)]
     offsets = [jnp.where(k >= 0, k - col * K_COL, -1) for k in columns]
-    bands = [jnp.clip(left_index[s, 0], 0, 1) for s in range(A_SLOTS)]
+    bands = [jnp.clip(left_index[0, s], 0, 1) for s in range(A_SLOTS)]
     write(left_out, offsets + bands)
     offsets = [right_index[s, 0] - row * K_ROW for s in range(B_SLOTS)]
     live = [o < K_ROW for o in offsets]
@@ -340,7 +340,7 @@
 
 
 def per_device(left_blocks, left_index, right_blocks, right_index, out_pattern):
-    left, right = pack(left_index, right_index, left_blocks, right_blocks)
+    left, right = pack(left_index.T, right_index, left_blocks, right_blocks)
     return multiply_parts(*gather(left, right), out_pattern)
 
 

time: 135 us -> 133 us (0.985)
    unnamed x18 -> x17, local copies, waits for them, and re-layouts: 6.65 us -> 5.32 us
where the time goes in v4:
time: 133 us; the launch traced here: 131 us
  starting transfers between devices  72.3 us (54%)
  waiting for transfers between devices  40.4 us (30%)
  Pallas kernels  9.93 us (7%)
  local copies, waits for them, and re-layouts  6.29 us (5%)
  other arithmetic  2 us (2%)
    ppermute x14, starting transfers between devices, swap(): return lax.ppermute(value, ('row', 'col'), pairs(partner))  72.3 us
    ppermute x14, waiting for transfers between devices, swap(): return lax.ppermute(value, ('row', 'col'), pairs(partner))  40.4 us
    pallas_call x1, Pallas kernels, multiply_parts(): pl.pallas_call(kernel, out_shape=jax.ShapeDtypeStruct((band * BLK, slab *...  6.45 us
    unnamed x17, local copies, waits for them, and re-layouts  5.32 us
  transfers between devices with their start and end apart: 14, of which 6 were waited for; matrix products, arithmetic and copies ran while one was open for 5% of the time, Pallas kernels for 1%

profile of v4, /device:TPU:1, one launch (start us, length us, event | category | flops | bytes accessed | tf_op | source)
XLA Modules:
  0.0 131.3 jit_solution(14930302303262651532)
XLA Ops:
  0.0 2.2 %pack.1 = (bf16[400,128]{1,0:T(8,128)(2,1)}, bf16[272,128]{1,0:T(8,128)(2,1)}) custom-call(s32[2,3]{1,0:T(2,128)} %bitcast.25, s32[2,2]{1,0:T(2,128)} %right_index.1, bf16[3,128,128]{2,1,0:T(8,128)(2,1)} %left_blocks.1, bf16[2,128,128]{2,1,0:T(8,128)(2,1)} %right_blocks.1), custom_call_target="tpu_custom_call" | custom-call | tf_op jit(solution)/shard_map/pack/pallas_call | solution.py:112
  2.2 9.8 %collective-permute-start.2 = (bf16[272,128]{1,0:T(8,128)(2,1)}, bf16[272,128]{1,0:T(8,128)(2,1)S(1)}, u32[]{:S(2)}, u32[]{:S(2)}) collective-permute-start(bf16[272,128]{1,0:T(8,128)(2,1)} %get-tuple-element.12), channel_id=1, source_target_pairs={{0,512},{1,513},{2,514},{3,515},{4,516},{5,517},{6,518},{7,519},{8... | collective-permute-start | bytes 208904 | tf_op jit(solution)/shard_map/ppermute | solution.py:38
  12.0 8.3 %collective-permute-start = (bf16[400,128]{1,0:T(8,128)(2,1)}, bf16[400,128]{1,0:T(8,128)(2,1)S(1)}, u32[]{:S(2)}, u32[]{:S(2)}) collective-permute-start(bf16[400,128]{1,0:T(8,128)(2,1)} %get-tuple-element.11), channel_id=1, source_target_pairs={{0,16},{1,17},{2,18},{3,19},{4,20},{5,21},{6,22},{7,23},{8,24},{9,... | collective-permute-start | bytes 307208 | tf_op jit(solution)/shard_map/ppermute | solution.py:38
  20.4 1.5 %constant_dynamic-update-slice_fusion.14 = (bf16[4352,128]{1,0:T(8,128)(2,1)}, bf16[2976,128]{1,0:T(8,128)(2,1)S(1)}) fusion(bf16[272,128]{1,0:T(8,128)(2,1)} %get-tuple-element.12), kind=kLoop, calls=%fused_computation.23 | loop fusion | bytes 208896
  21.9 0.9 constant_dynamic-update-slice_fusion.9
  22.8 0.9 pad_maximum_fusion.7
  23.7 1.9 %collective-permute-start.3 = (bf16[544,128]{1,0:T(8,128)(2,1)S(1)}, bf16[544,128]{1,0:T(8,128)(2,1)S(1)}, u32[]{:S(2)}, u32[]{:S(2)}) collective-permute-start(bf16[544,128]{1,0:T(8,128)(2,1)S(1)} %pad_maximum_fusion.7), channel_id=1, source_target_pairs={{0,256},{1,257},{2,258},{3,259},{4,260},{5,261},{6,262},{7,263},{8... | collective-permute-start | bytes 417800 | tf_op jit(solution)/shard_map/ppermute | solution.py:38
  25.6 0.6 constant_dynamic-update-slice_fusion.13
  26.3 0.9 pad_maximum_fusion.6
  27.2 17.2 %collective-permute-start.1 = (bf16[800,128]{1,0:T(8,128)(2,1)S(1)}, bf16[800,128]{1,0:T(8,128)(2,1)S(1)}, u32[]{:S(2)}, u32[]{:S(2)}) collective-permute-start(bf16[800,128]{1,0:T(8,128)(2,1)S(1)} %pad_maximum_fusion.6), channel_id=1, source_target_pairs={{0,1},{1,0},{2,3},{3,2},{4,5},{5,4},{6,7},{7,6},{8,9},{9,8},{10,11... | collective-permute-start | bytes 614408 | tf_op jit(solution)/shard_map/ppermute | solution.py:38
  44.5 1.9 %collective-permute-start.4 = (bf16[1088,128]{1,0:T(8,128)(2,1)S(1)}, bf16[1088,128]{1,0:T(8,128)(2,1)S(1)}, u32[]{:S(2)}, u32[]{:S(2)}) collective-permute-start(bf16[1088,128]{1,0:T(8,128)(2,1)S(1)} %pad_maximum_fusion.5), channel_id=1, source_target_pairs={{0,128},{1,129},{2,130},{3,131},{4,132},{5,133},{6,134},{7,135},{8... | collective-permute-start | bytes 835592 | tf_op jit(solution)/shard_map/ppermute | solution.py:38
  46.4 0.7 constant_dynamic-update-slice_fusion.12
  47.1 7.9 %collective-permute-done.1 = bf16[800,128]{1,0:T(8,128)(2,1)S(1)} collective-permute-done((bf16[800,128]{1,0:T(8,128)(2,1)S(1)}, bf16[800,128]{1,0:T(8,128)(2,1)S(1)}, u32[]{:S(2)}, u32[]{:S(2)}) %collective-permute-start.1) | collective-permute-done | bytes 204832 | tf_op jit(solution)/shard_map/ppermute | solution.py:38
  55.0 0.6 slice.60.in_ref
  55.5 1.3 hold.1
  56.8 11.3 %collective-permute-done.4 = bf16[1088,128]{1,0:T(8,128)(2,1)S(1)} collective-permute-done((bf16[1088,128]{1,0:T(8,128)(2,1)S(1)}, bf16[1088,128]{1,0:T(8,128)(2,1)S(1)}, u32[]{:S(2)}, u32[]{:S(2)}) %collective-permute-start.4) | collective-permute-done | bytes 278560 | tf_op jit(solution)/shard_map/ppermute | solution.py:38
  68.2 0.8 constant_dynamic-update-slice_fusion.11
  68.9 0.8 constant_dynamic-update-slice_fusion.8
  69.7 1.9 %collective-permute-start.5 = (bf16[2976,128]{1,0:T(8,128)(2,1)S(1)}, bf16[2976,128]{1,0:T(8,128)(2,1)S(1)}, u32[]{:S(2)}, u32[]{:S(2)}) collective-permute-start(bf16[2976,128]{1,0:T(8,128)(2,1)S(1)} %slice_dynamic-update-slice_fusion), channel_id=1, source_target_pairs={{0,16},{1,17},{2,18},{3,19},{4,20},{5,21},{6,22},{7,23},{8,24},{9,... | collective-permute-start | bytes 2285576 | tf_op jit(solution)/shard_map/ppermute | solution.py:38
  71.7 6.5 %collective-permute-start.6 = (bf16[400,128]{1,0:T(8,128)(2,1)S(1)}, bf16[400,128]{1,0:T(8,128)(2,1)S(1)}, u32[]{:S(2)}, u32[]{:S(2)}) collective-permute-start(bf16[400,128]{1,0:T(8,128)(2,1)S(1)} %get-tuple-element.26), channel_id=1, source_target_pairs={{0,3},{1,2},{2,1},{3,0},{4,7},{5,6},{6,5},{7,4},{8,11},{9,10},{10,... | collective-permute-start | bytes 307208 | tf_op jit(solution)/shard_map/ppermute | solution.py:38
  78.3 4.4 %collective-permute-start.10 = (bf16[4352,128]{1,0:T(8,128)(2,1)S(1)}, bf16[4352,128]{1,0:T(8,128)(2,1)S(1)}, u32[]{:S(2)}, u32[]{:S(2)}) collective-permute-start(bf16[4352,128]{1,0:T(8,128)(2,1)S(1)} %get-tuple-element.18), channel_id=1, source_target_pairs={{0,32},{1,33},{2,34},{3,35},{4,36},{5,37},{6,38},{7,39},{8,40},{9,... | collective-permute-start | bytes 3342344 | tf_op jit(solution)/shard_map/ppermute | solution.py:38
  82.8 8.6 %collective-permute-done.6 = bf16[400,128]{1,0:T(8,128)(2,1)S(1)} collective-permute-done((bf16[400,128]{1,0:T(8,128)(2,1)S(1)}, bf16[400,128]{1,0:T(8,128)(2,1)S(1)}, u32[]{:S(2)}, u32[]{:S(2)}) %collective-permute-start.6) | collective-permute-done | bytes 102432 | tf_op jit(solution)/shard_map/ppermute | solution.py:38
  91.4 4.2 %collective-permute-start.7 = (bf16[2400,128]{1,0:T(8,128)(2,1)S(1)}, bf16[2400,128]{1,0:T(8,128)(2,1)S(1)}, u32[]{:S(2)}, u32[]{:S(2)}) collective-permute-start(bf16[2400,128]{1,0:T(8,128)(2,1)S(1)} %constant_dynamic-update-slice_fusion.5), channel_id=1, source_target_pairs={{0,4},{1,5},{2,6},{3,7},{4,0},{5,1},{6,2},{7,3},{8,12},{9,13},{10,... | collective-permute-start | bytes 1843208 | tf_op jit(solution)/shard_map/ppermute | solution.py:38
  95.6 2.3 %collective-permute-start.8 = (bf16[400,128]{1,0:T(8,128)(2,1)S(1)}, bf16[400,128]{1,0:T(8,128)(2,1)S(1)}, u32[]{:S(2)}, u32[]{:S(2)}) collective-permute-start(bf16[400,128]{1,0:T(8,128)(2,1)S(1)} %collective-permute-done.6), channel_id=1, source_target_pairs={{0,4},{1,5},{2,6},{3,7},{4,0},{5,1},{6,2},{7,3},{8,12},{9,13},{10,... | collective-permute-start | bytes 307208 | tf_op jit(solution)/shard_map/ppermute | solution.py:38
  98.0 2.7 %collective-permute-start.11 = (bf16[2176,128]{1,0:T(8,128)(2,1)S(1)}, bf16[2176,128]{1,0:T(8,128)(2,1)S(1)}, u32[]{:S(2)}, u32[]{:S(2)}) collective-permute-start(bf16[2176,128]{1,0:T(8,128)(2,1)S(1)} %slice.68), channel_id=1, source_target_pairs={{0,96},{1,97},{2,98},{3,99},{4,100},{5,101},{6,102},{7,103},{8,104... | collective-permute-start | bytes 1671176 | tf_op jit(solution)/shard_map/ppermute | solution.py:38
  100.7 3.9 %collective-permute-done.8 = bf16[400,128]{1,0:T(8,128)(2,1)S(1)} collective-permute-done((bf16[400,128]{1,0:T(8,128)(2,1)S(1)}, bf16[400,128]{1,0:T(8,128)(2,1)S(1)}, u32[]{:S(2)}, u32[]{:S(2)}) %collective-permute-start.8) | collective-permute-done | bytes 102432 | tf_op jit(solution)/shard_map/ppermute | solution.py:38
  104.7 1.9 %collective-permute-start.13 = (bf16[4352,128]{1,0:T(8,128)(2,1)S(1)}, bf16[4352,128]{1,0:T(8,128)(2,1)S(1)}, u32[]{:S(2)}, u32[]{:S(2)}) collective-permute-start(bf16[4352,128]{1,0:T(8,128)(2,1)S(1)} %collective-permute-done.10), channel_id=1, source_target_pairs={{0,16},{1,17},{2,18},{3,19},{4,20},{5,21},{6,22},{7,23},{8,24},{9,... | collective-permute-start | bytes 3342344 | tf_op jit(solution)/shard_map/ppermute | solution.py:38
  106.6 2.0 %collective-permute-done.11 = bf16[2176,128]{1,0:T(8,128)(2,1)S(1)} collective-permute-done((bf16[2176,128]{1,0:T(8,128)(2,1)S(1)}, bf16[2176,128]{1,0:T(8,128)(2,1)S(1)}, u32[]{:S(2)}, u32[]{:S(2)}) %collective-permute-start.11) | collective-permute-done | bytes 557088 | tf_op jit(solution)/shard_map/ppermute | solution.py:38
  108.6 6.0 %collective-permute-start.12 = (bf16[3376,128]{1,0:T(8,128)(2,1)S(1)}, bf16[3376,128]{1,0:T(8,128)(2,1)S(1)}, u32[]{:S(2)}, u32[]{:S(2)}) collective-permute-start(bf16[3376,128]{1,0:T(8,128)(2,1)S(1)} %pad_maximum_fusion), channel_id=1, source_target_pairs={{0,16},{1,17},{2,18},{3,19},{4,20},{5,21},{6,22},{7,23},{8,24},{9,... | collective-permute-start | bytes 2592776 | tf_op jit(solution)/shard_map/ppermute | solution.py:38
  114.7 3.2 %collective-permute-start.9 = (bf16[2000,128]{1,0:T(8,128)(2,1)S(1)}, bf16[2000,128]{1,0:T(8,128)(2,1)S(1)}, u32[]{:S(2)}, u32[]{:S(2)}) collective-permute-start(bf16[2000,128]{1,0:T(8,128)(2,1)S(1)} %pad_maximum_fusion.2), channel_id=1, source_target_pairs={{0,12},{1,13},{2,14},{3,15},{4,8},{5,9},{6,10},{7,11},{8,4},{9,5},... | collective-permute-start | bytes 1536008 | tf_op jit(solution)/shard_map/ppermute | solution.py:38
  118.1 6.7 %collective-permute-done.9 = bf16[2000,128]{1,0:T(8,128)(2,1)S(1)} collective-permute-done((bf16[2000,128]{1,0:T(8,128)(2,1)S(1)}, bf16[2000,128]{1,0:T(8,128)(2,1)S(1)}, u32[]{:S(2)}, u32[]{:S(2)}) %collective-permute-start.9) | collective-permute-done | bytes 512032 | tf_op jit(solution)/shard_map/ppermute | solution.py:38
  124.8 6.4 %block_products.1 = bf16[256,1024]{1,0:T(8,128)(2,1)} custom-call(s32[2,8]{1,0:T(2,128)S(1)} %copy-done, bf16[3,400,128]{2,1,0:T(8,128)(2,1)S(1)} %bitcast.19, bf16[3,400,128]{2,1,0:T(8,128)(2,1)S(1)} %bitcast.13, bf16[5,400,128]{2,1,0:T(8,128)(2,1)S(1)} %bitcast.22, bf16[3,400,128]{2,1,0:T(8,128)(2,1)S(1)} %bitcast.20, bf16[1,400,128]{2,1,0:T(8,128)(2,1)S(1)} %bitcast.23, ...), custom_call_target="tpu_custom_call" | custom-call | tf_op jit(solution)/shard_map/block_products/pallas_call | solution.py:317
  (34 shorter events, 0.6 us)
Async XLA Ops:
  2.2 42.2 %copy-start.1 = (bf16[272,128]{1,0:T(8,128)(2,1)S(1)}, bf16[272,128]{1,0:T(8,128)(2,1)}, u32[]{:S(2)}) copy-start(bf16[272,128]{1,0:T(8,128)(2,1)} %get-tuple-element.12) | copy-start | bytes 208900
  2.2 20.6 %collective-permute-start.2 = (bf16[272,128]{1,0:T(8,128)(2,1)}, bf16[272,128]{1,0:T(8,128)(2,1)S(1)}, u32[]{:S(2)}, u32[]{:S(2)}) collective-permute-start(bf16[272,128]{1,0:T(8,128)(2,1)} %get-tuple-element.12), channel_id=1, source_target_pairs={{0,512},{1,513},{2,514},{3,515},{4,516},{5,517},{6,518},{7,519},{8... | collective-permute-start | bytes 208904 | tf_op jit(solution)/shard_map/ppermute | solution.py:38
  12.0 14.2 %collective-permute-start = (bf16[400,128]{1,0:T(8,128)(2,1)}, bf16[400,128]{1,0:T(8,128)(2,1)S(1)}, u32[]{:S(2)}, u32[]{:S(2)}) collective-permute-start(bf16[400,128]{1,0:T(8,128)(2,1)} %get-tuple-element.11), channel_id=1, source_target_pairs={{0,16},{1,17},{2,18},{3,19},{4,20},{5,21},{6,22},{7,23},{8,24},{9,... | collective-permute-start | bytes 307208 | tf_op jit(solution)/shard_map/ppermute | solution.py:38
  23.7 20.7 %collective-permute-start.3 = (bf16[544,128]{1,0:T(8,128)(2,1)S(1)}, bf16[544,128]{1,0:T(8,128)(2,1)S(1)}, u32[]{:S(2)}, u32[]{:S(2)}) collective-permute-start(bf16[544,128]{1,0:T(8,128)(2,1)S(1)} %pad_maximum_fusion.7), channel_id=1, source_target_pairs={{0,256},{1,257},{2,258},{3,259},{4,260},{5,261},{6,262},{7,263},{8... | collective-permute-start | bytes 417800 | tf_op jit(solution)/shard_map/ppermute | solution.py:38
  27.2 27.8 %collective-permute-start.1 = (bf16[800,128]{1,0:T(8,128)(2,1)S(1)}, bf16[800,128]{1,0:T(8,128)(2,1)S(1)}, u32[]{:S(2)}, u32[]{:S(2)}) collective-permute-start(bf16[800,128]{1,0:T(8,128)(2,1)S(1)} %pad_maximum_fusion.6), channel_id=1, source_target_pairs={{0,1},{1,0},{2,3},{3,2},{4,5},{5,4},{6,7},{7,6},{8,9},{9,8},{10,11... | collective-permute-start | bytes 614408 | tf_op jit(solution)/shard_map/ppermute | solution.py:38
  44.5 23.7 %collective-permute-start.4 = (bf16[1088,128]{1,0:T(8,128)(2,1)S(1)}, bf16[1088,128]{1,0:T(8,128)(2,1)S(1)}, u32[]{:S(2)}, u32[]{:S(2)}) collective-permute-start(bf16[1088,128]{1,0:T(8,128)(2,1)S(1)} %pad_maximum_fusion.5), channel_id=1, source_target_pairs={{0,128},{1,129},{2,130},{3,131},{4,132},{5,133},{6,134},{7,135},{8... | collective-permute-start | bytes 835592 | tf_op jit(solution)/shard_map/ppermute | solution.py:38
  68.9 9.3 %copy-start.4 = (bf16[4352,128]{1,0:T(8,128)(2,1)S(1)}, bf16[4352,128]{1,0:T(8,128)(2,1)}, u32[]{:S(2)}) copy-start(bf16[4352,128]{1,0:T(8,128)(2,1)} %get-tuple-element.24) | copy-start | bytes 3342340
  69.7 8.4 %collective-permute-start.5 = (bf16[2976,128]{1,0:T(8,128)(2,1)S(1)}, bf16[2976,128]{1,0:T(8,128)(2,1)S(1)}, u32[]{:S(2)}, u32[]{:S(2)}) collective-permute-start(bf16[2976,128]{1,0:T(8,128)(2,1)S(1)} %slice_dynamic-update-slice_fusion), channel_id=1, source_target_pairs={{0,16},{1,17},{2,18},{3,19},{4,20},{5,21},{6,22},{7,23},{8,24},{9,... | collective-permute-start | bytes 2285576 | tf_op jit(solution)/shard_map/ppermute | solution.py:38
  71.7 19.7 %collective-permute-start.6 = (bf16[400,128]{1,0:T(8,128)(2,1)S(1)}, bf16[400,128]{1,0:T(8,128)(2,1)S(1)}, u32[]{:S(2)}, u32[]{:S(2)}) collective-permute-start(bf16[400,128]{1,0:T(8,128)(2,1)S(1)} %get-tuple-element.26), channel_id=1, source_target_pairs={{0,3},{1,2},{2,1},{3,0},{4,7},{5,6},{6,5},{7,4},{8,11},{9,10},{10,... | collective-permute-start | bytes 307208 | tf_op jit(solution)/shard_map/ppermute | solution.py:38
  78.3 19.6 %collective-permute-start.10 = (bf16[4352,128]{1,0:T(8,128)(2,1)S(1)}, bf16[4352,128]{1,0:T(8,128)(2,1)S(1)}, u32[]{:S(2)}, u32[]{:S(2)}) collective-permute-start(bf16[4352,128]{1,0:T(8,128)(2,1)S(1)} %get-tuple-element.18), channel_id=1, source_target_pairs={{0,32},{1,33},{2,34},{3,35},{4,36},{5,37},{6,38},{7,39},{8,40},{9,... | collective-permute-start | bytes 3342344 | tf_op jit(solution)/shard_map/ppermute | solution.py:38
  91.4 13.2 %collective-permute-start.7 = (bf16[2400,128]{1,0:T(8,128)(2,1)S(1)}, bf16[2400,128]{1,0:T(8,128)(2,1)S(1)}, u32[]{:S(2)}, u32[]{:S(2)}) collective-permute-start(bf16[2400,128]{1,0:T(8,128)(2,1)S(1)} %constant_dynamic-update-slice_fusion.5), channel_id=1, source_target_pairs={{0,4},{1,5},{2,6},{3,7},{4,0},{5,1},{6,2},{7,3},{8,12},{9,13},{10,... | collective-permute-start | bytes 1843208 | tf_op jit(solution)/shard_map/ppermute | solution.py:38
  95.6 9.0 %collective-permute-start.8 = (bf16[400,128]{1,0:T(8,128)(2,1)S(1)}, bf16[400,128]{1,0:T(8,128)(2,1)S(1)}, u32[]{:S(2)}, u32[]{:S(2)}) collective-permute-start(bf16[400,128]{1,0:T(8,128)(2,1)S(1)} %collective-permute-done.6), channel_id=1, source_target_pairs={{0,4},{1,5},{2,6},{3,7},{4,0},{5,1},{6,2},{7,3},{8,12},{9,13},{10,... | collective-permute-start | bytes 307208 | tf_op jit(solution)/shard_map/ppermute | solution.py:38
  98.0 10.6 %collective-permute-start.11 = (bf16[2176,128]{1,0:T(8,128)(2,1)S(1)}, bf16[2176,128]{1,0:T(8,128)(2,1)S(1)}, u32[]{:S(2)}, u32[]{:S(2)}) collective-permute-start(bf16[2176,128]{1,0:T(8,128)(2,1)S(1)} %slice.68), channel_id=1, source_target_pairs={{0,96},{1,97},{2,98},{3,99},{4,100},{5,101},{6,102},{7,103},{8,104... | collective-permute-start | bytes 1671176 | tf_op jit(solution)/shard_map/ppermute | solution.py:38
  104.7 20.1 %collective-permute-start.13 = (bf16[4352,128]{1,0:T(8,128)(2,1)S(1)}, bf16[4352,128]{1,0:T(8,128)(2,1)S(1)}, u32[]{:S(2)}, u32[]{:S(2)}) collective-permute-start(bf16[4352,128]{1,0:T(8,128)(2,1)S(1)} %collective-permute-done.10), channel_id=1, source_target_pairs={{0,16},{1,17},{2,18},{3,19},{4,20},{5,21},{6,22},{7,23},{8,24},{9,... | collective-permute-start | bytes 3342344 | tf_op jit(solution)/shard_map/ppermute | solution.py:38
  108.6 9.4 %copy-start.2 = (bf16[400,128]{1,0:T(8,128)(2,1)S(1)}, bf16[400,128]{1,0:T(8,128)(2,1)}, u32[]{:S(2)}) copy-start(bf16[400,128]{1,0:T(8,128)(2,1)} %get-tuple-element.11) | copy-start | bytes 307204
  108.6 9.4 %copy-start.3 = (bf16[16,128]{1,0:T(8,128)(2,1)S(1)}, bf16[16,128]{1,0:T(8,128)(2,1)}, u32[]{:S(2)}) copy-start(bf16[16,128]{1,0:T(8,128)(2,1)} %hold.1) | copy-start | bytes 12292
  108.6 9.4 %collective-permute-start.12 = (bf16[3376,128]{1,0:T(8,128)(2,1)S(1)}, bf16[3376,128]{1,0:T(8,128)(2,1)S(1)}, u32[]{:S(2)}, u32[]{:S(2)}) collective-permute-start(bf16[3376,128]{1,0:T(8,128)(2,1)S(1)} %pad_maximum_fusion), channel_id=1, source_target_pairs={{0,16},{1,17},{2,18},{3,19},{4,20},{5,21},{6,22},{7,23},{8,24},{9,... | collective-permute-start | bytes 2592776 | tf_op jit(solution)/shard_map/ppermute | solution.py:38
  114.7 10.1 %collective-permute-start.9 = (bf16[2000,128]{1,0:T(8,128)(2,1)S(1)}, bf16[2000,128]{1,0:T(8,128)(2,1)S(1)}, u32[]{:S(2)}, u32[]{:S(2)}) collective-permute-start(bf16[2000,128]{1,0:T(8,128)(2,1)S(1)} %pad_maximum_fusion.2), channel_id=1, source_target_pairs={{0,12},{1,13},{2,14},{3,15},{4,8},{5,9},{6,10},{7,11},{8,4},{9,5},... | collective-permute-start | bytes 1536008 | tf_op jit(solution)/shard_map/ppermute | solution.py:38
  118.0 6.8 %copy-start = (s32[2,8]{1,0:T(2,128)S(1)}, s32[2,8]{1,0:T(2,128)}, u32[]{:S(2)}) copy-start(s32[2,8]{1,0:T(2,128)} %refs_0_.1) | copy-start | bytes 196
